TPU v7x, 32 devices: a whole 2x2x4 slice. The times are simulated.
32 devices in a mesh: groups: 2 (over x), seq: 16 (over z, y, core).
Axes of the slice: x: 2, y: 2, z: 4, core: 2. Of those that a mesh axis runs over, the one named last changes fastest.
Arguments:
- atom_features: bfloat16 [4, 8192, 256], P('groups', 'seq'), parts along dimension 0, may hold values from -6 to 6
- cotangent: bfloat16 [4, 8192, 256], P('groups', 'seq'), parts along dimension 0, may hold values from -6 to 6
- charge_weight: bfloat16 [256, 16], replicated, may hold values from -0.375 to 0.375
- message_weight: bfloat16 [16, 256], replicated, may hold values from -1.5 to 1.5
- amplitude: float32 [16], replicated, may hold values from 1 to 4
- smoothing: float32 [16], replicated, may hold values from 0.5 to 2
- screening: float32 [16], replicated, may hold values from 0.05 to 0.15
- base_cells: int32 [4, 3, 8192], P('groups', None, 'seq'), parts along dimension 0, may hold values from 0 to 63, as said below
- cell_offsets: float32 [4, 3, 8192], P('groups', None, 'seq'), parts along dimension 0, may hold values from 0 to 1
- row_starts: int32 [4, 64], P('groups', 'seq'), parts along dimension 0, may hold values from 0 to 56, as said below
- block_counts: int32 [4, 64], P('groups', 'seq'), parts along dimension 0, may hold values from 1 to 128, 7168 in all within a row
Outputs:
- message: bfloat16 [4, 8192, 256], P('groups', 'seq'), parts along dimension 0
- atom_gradient: bfloat16 [4, 8192, 256], P('groups', 'seq'), parts along dimension 0
- gradient_in: float32 [512, 16], P('groups'), parts along dimension 0
- gradient_out: float32 [32, 256], P('groups'), parts along dimension 0
- filter_gradient: float32 [6, 16], P('groups'), parts along dimension 0
There are 2 independent parts, one for each index of `groups`. A program takes and returns all parts, laid end to end along the dimension named above; an argument that names none is the same for every part. Nothing has to cross between parts.
Inputs may be any that keep to these rules, and one draw needn't show every extreme that they name: `base_cells`: an atom in block b held by seq index d (blocks d * 4 to (d + 1) * 4 - 1) has its depth base in [d * 4, (d + 1) * 4) and its row base equal to (row_starts of block b + r) mod 64 with 0 <= r <= 28; its column base is any cell. `row_starts`: each block's first brick row is a multiple of 8. `block_counts`: slots of a block below its count hold atoms, the others are padding.
All inputs are finite; a program needn't handle non-finite values.
Results may differ from a plain program's by a relative error of at most 0.0068.
Values may be sent and summed in bfloat16 or wider, within the bound.
A program may use at most 128 MiB of HBM per device.

v0:
```python
import functools
import math

import jax
import jax.numpy as jnp
import ml_dtypes
import numpy as np
from jax import lax
from jax.experimental import pallas as pl
from jax.experimental.pallas import tpu as pltpu
from jax.sharding import PartitionSpec as P

M = 64
BAND = 32


def passed_along(value, axis, by):
    count = lax.axis_size(axis)
    return lax.ppermute(value, axis, [(i, (i + by) % count) for i in range(count)])


def spline_weights(fraction):
    remain = 1.0 - fraction
    square = fraction * fraction
    cubed = square * fraction
    return (
        remain * remain * remain / 6.0,
        (3.0 * cubed - 6.0 * square + 4.0) / 6.0,
        (-3.0 * cubed + 3.0 * square + 3.0 * fraction + 1.0) / 6.0,
        cubed / 6.0,
    )


def pick_weight(lattice_gap, weights):
    picked = jnp.where(lattice_gap == 0, weights[0], 0.0)
    for order_index in range(1, 4):
        picked = picked + jnp.where(lattice_gap == order_index, weights[order_index], 0.0)
    return picked


def atom_weights(base_cells, cell_offsets, row_start, plane_start, plane_count):
    atom_count = base_cells.shape[1]
    depth_index = plane_start + jnp.arange(plane_count, dtype=jnp.int32)
    row_index = row_start + jnp.arange(BAND, dtype=jnp.int32)
    column_index = jnp.arange(M, dtype=jnp.int32)
    along_depth = pick_weight(
        (depth_index[None, :] - base_cells[0][:, None]) % M,
        spline_weights(cell_offsets[0][:, None]),
    )
    along_rows = pick_weight(
        (row_index[None, :] - base_cells[1][:, None]) % M, spline_weights(cell_offsets[1][:, None])
    )
    along_columns = pick_weight(
        (column_index[None, :] - base_cells[2][:, None]) % M,
        spline_weights(cell_offsets[2][:, None]),
    )
    plane_rows = (
        (along_depth[:, :, None] * along_rows[:, None, :])
        .reshape(atom_count, plane_count * BAND)
        .astype(jnp.bfloat16)
    )
    return (plane_rows, along_columns)


def hartley_table():
    indices = jnp.arange(M, dtype=jnp.int32)
    product = indices[:, None] * indices[None, :] % M
    angles = product.astype(jnp.float32) * (2.0 * math.pi / M)
    return jnp.cos(angles) + jnp.sin(angles)


def wave_numbers(indices):
    return jnp.where(indices < M // 2, indices, indices - M).astype(jnp.float32) * (
        2.0 * math.pi / M
    )


def squared_waves(row_first, row_count):
    depth_waves = wave_numbers(jnp.arange(M, dtype=jnp.int32))
    row_waves = wave_numbers(row_first + jnp.arange(row_count, dtype=jnp.int32))
    summed = (
        depth_waves[:, None, None] ** 2
        + row_waves[None, :, None] ** 2
        + depth_waves[None, None, :] ** 2
    )
    return summed[:, :, None, :]


def scaled_filter(amplitude, smoothing, screening, wave_square):
    gains = amplitude[None, None, :, None]
    widths = (smoothing * smoothing)[None, None, :, None]
    screens = (screening * screening)[None, None, :, None]
    return gains * jnp.exp(-0.5 * widths * wave_square) / (wave_square + screens) * (1.0 / M**3)


def spread_cell(charges, base_cells, cell_offsets, row_starts, plane_start, plane_count):
    blocks = row_starts.shape[0]
    atom_count = charges.shape[0] // blocks
    columns = charges.shape[1] * M

    def add_block(padded, block_index):
        first_row = block_index * atom_count
        block_charges = lax.dynamic_slice_in_dim(charges, first_row, atom_count, 0)
        block_cells = lax.dynamic_slice_in_dim(base_cells, first_row, atom_count, 1)
        block_offsets = lax.dynamic_slice_in_dim(cell_offsets, first_row, atom_count, 1)
        row_start = row_starts[block_index]
        plane_rows, along_columns = atom_weights(
            block_cells, block_offsets, row_start, plane_start, plane_count
        )
        spread_rows = (
            (block_charges.astype(jnp.float32)[:, :, None] * along_columns[:, None, :])
            .reshape(atom_count, columns)
            .astype(jnp.bfloat16)
        )
        addition = lax.dot_general(
            plane_rows, spread_rows, (((0,), (0,)), ((), ())), preferred_element_type=jnp.float32
        )
        addition = addition.reshape(plane_count, BAND, columns)
        current = lax.dynamic_slice_in_dim(padded, row_start, BAND, 1)
        return (lax.dynamic_update_slice_in_dim(padded, current + addition, row_start, 1), None)

    padded = jnp.zeros((plane_count, M + BAND, columns), jnp.float32)
    padded, unused = lax.scan(add_block, padded, jnp.arange(blocks, dtype=jnp.int32))
    return padded[:, :M].at[:, :BAND].add(padded[:, M:])


def interpolate_cell(mesh, base_cells, cell_offsets, row_starts, plane_start):
    plane_count = mesh.shape[0]
    blocks = row_starts.shape[0]
    atom_count = base_cells.shape[1] // blocks
    padded = jnp.concatenate([mesh, mesh[:, :BAND]], axis=1)

    def one_block(block_index):
        first_row = block_index * atom_count
        block_cells = lax.dynamic_slice_in_dim(base_cells, first_row, atom_count, 1)
        block_offsets = lax.dynamic_slice_in_dim(cell_offsets, first_row, atom_count, 1)
        row_start = row_starts[block_index]
        plane_rows, along_columns = atom_weights(
            block_cells, block_offsets, row_start, plane_start, plane_count
        )
        window = lax.dynamic_slice_in_dim(padded, row_start, BAND, 1).reshape(
            plane_count * BAND, -1
        )
        values = jnp.dot(plane_rows, window, preferred_element_type=jnp.float32)
        return jnp.sum(values.reshape(atom_count, -1, M) * along_columns[:, None, :], axis=2)

    return lax.map(one_block, jnp.arange(blocks, dtype=jnp.int32)).reshape(blocks * atom_count, -1)


def spread_cells(charges, base_cells, cell_offsets, row_starts, plane_start, plane_count):

    def spread_one_cell(cell_data):
        return spread_cell(
            cell_data[0], cell_data[1], cell_data[2], cell_data[3], plane_start, plane_count
        )

    return lax.map(spread_one_cell, (charges, base_cells, cell_offsets, row_starts))


def interpolate_cells(mesh, base_cells, cell_offsets, row_starts, plane_start):

    def interpolate_one_cell(cell_data):
        return interpolate_cell(cell_data[0], cell_data[1], cell_data[2], cell_data[3], plane_start)

    return lax.map(interpolate_one_cell, (mesh, base_cells, cell_offsets, row_starts))


def long_range(charges, base_cells, cell_offsets, row_starts, spectral_filter):
    devices = lax.axis_size("seq")
    planes = M // devices
    spill_reach = (planes + 2) // planes
    plane_start = lax.axis_index("seq") * planes
    cell_count = charges.shape[0]
    channels = charges.shape[2]
    hartley = hartley_table()
    highest = lax.Precision.HIGHEST
    extended = spread_cells(charges, base_cells, cell_offsets, row_starts, plane_start, planes + 3)
    mesh_field = extended[:, :planes]
    for distance in range(1, spill_reach + 1):
        lower_plane = (distance - 1) * planes
        upper_plane = min(distance * planes, 3)
        arrived = passed_along(
            extended[:, planes + lower_plane : planes + upper_plane], "seq", distance
        )
        mesh_field = mesh_field.at[:, : upper_plane - lower_plane].add(arrived)
    slab_data = mesh_field.reshape(cell_count, planes, M, channels, M)
    spectrum = jnp.einsum("kpycx,xf->kpycf", slab_data, hartley, precision=highest)
    spectrum = jnp.einsum("kpycx,yf->kpfcx", spectrum, hartley, precision=highest)
    forward = jnp.einsum(
        "kzycx,zf->kfycx",
        lax.all_to_all(spectrum, "seq", split_axis=2, concat_axis=1, tiled=True),
        hartley,
        precision=highest,
    )
    weighted = spectral_filter[None] * forward
    returned = jnp.einsum("kzycx,zf->kfycx", weighted, hartley, precision=highest)
    slab_back = lax.all_to_all(returned, "seq", split_axis=1, concat_axis=2, tiled=True)
    slab_back = jnp.einsum("kpycx,yf->kpfcx", slab_back, hartley, precision=highest)
    slab_back = jnp.einsum("kpycx,xf->kpycf", slab_back, hartley, precision=highest)
    rounded = slab_back.reshape(cell_count, planes, M, channels * M).astype(jnp.bfloat16)
    pieces = [rounded]
    for distance in range(1, spill_reach + 1):
        lower_plane = (distance - 1) * planes
        upper_plane = min(distance * planes, 3)
        pieces.append(passed_along(rounded[:, : upper_plane - lower_plane], "seq", -distance))
    values = interpolate_cells(
        jnp.concatenate(pieces, axis=1), base_cells, cell_offsets, row_starts, plane_start
    )
    return (values, forward)


def on_device(
    atom_features,
    cotangent,
    charge_weight,
    message_weight,
    amplitude,
    smoothing,
    screening,
    base_cells,
    cell_offsets,
    row_starts,
    block_counts,
):
    cell_count, atom_rows, features = atom_features.shape
    channels = charge_weight.shape[1]
    devices = lax.axis_size("seq")
    blocks = block_counts.shape[1]
    slot_index = jnp.arange(atom_rows // blocks, dtype=jnp.int32)
    live_mask = (
        (slot_index[None, None, :] < block_counts[:, :, None])
        .reshape(cell_count, atom_rows)
        .astype(jnp.float32)
    )
    projected = jnp.dot(
        atom_features.reshape(-1, features), charge_weight, preferred_element_type=jnp.float32
    )
    charges = (live_mask[:, :, None] * projected.reshape(cell_count, atom_rows, channels)).astype(
        jnp.bfloat16
    )
    pulled = lax.dot_general(
        cotangent.reshape(-1, features),
        message_weight,
        (((1,), (1,)), ((), ())),
        preferred_element_type=jnp.float32,
    )
    adjoint = (live_mask[:, :, None] * pulled.reshape(cell_count, atom_rows, channels)).astype(
        jnp.bfloat16
    )
    row_count = M // devices
    wave_square = squared_waves(lax.axis_index("seq") * row_count, row_count)
    spectral_filter = scaled_filter(amplitude, smoothing, screening, wave_square)
    potential, source_spectra = long_range(
        charges, base_cells, cell_offsets, row_starts, spectral_filter
    )
    response, adjoint_spectra = long_range(
        adjoint, base_cells, cell_offsets, row_starts, spectral_filter
    )
    potential_rounded = potential.astype(jnp.bfloat16)
    outgoing = jnp.dot(
        potential_rounded.reshape(-1, channels), message_weight, preferred_element_type=jnp.float32
    )
    message = (live_mask[:, :, None] * outgoing.reshape(cell_count, atom_rows, features)).astype(
        jnp.bfloat16
    )
    response_rounded = (live_mask[:, :, None] * response).astype(jnp.bfloat16)
    backward = lax.dot_general(
        response_rounded.reshape(-1, channels),
        charge_weight,
        (((1,), (1,)), ((), ())),
        preferred_element_type=jnp.float32,
    )
    atom_gradient = backward.reshape(cell_count, atom_rows, features).astype(jnp.bfloat16)
    gradient_scale = 1.0 / math.sqrt(cell_count * atom_rows * devices)
    masked_cotangent = jnp.where(live_mask[:, :, None] > 0, cotangent, jnp.zeros((), jnp.bfloat16))
    gradient_in = (
        lax.dot_general(
            atom_features.reshape(-1, features),
            response_rounded.reshape(-1, channels),
            (((0,), (0,)), ((), ())),
            preferred_element_type=jnp.float32,
        )
        * gradient_scale
    )
    gradient_out = (
        lax.dot_general(
            potential_rounded.reshape(-1, channels),
            masked_cotangent.reshape(-1, features),
            (((0,), (0,)), ((), ())),
            preferred_element_type=jnp.float32,
        )
        * gradient_scale
    )
    intersection = jnp.sum(source_spectra * adjoint_spectra, axis=0) * spectral_filter
    widths = (smoothing * smoothing)[None, None, :, None]
    screens = (screening * screening)[None, None, :, None]
    smooth_factor = -widths * wave_square
    screen_factor = -2.0 * screens / (wave_square + screens)
    filter_terms = (
        jnp.stack(
            [
                jnp.sum(intersection, axis=(0, 1, 3)),
                jnp.sum(intersection * smooth_factor, axis=(0, 1, 3)),
                jnp.sum(intersection * screen_factor, axis=(0, 1, 3)),
            ]
        )
        * gradient_scale
    )
    gradient_in, gradient_out, filter_terms = lax.psum(
        (gradient_in, gradient_out, filter_terms), "seq"
    )
    return (message, atom_gradient, gradient_in, gradient_out, filter_terms)


def stacked_tables(planes):
    indices = np.arange(M)
    angles = (indices[:, None] * indices[None, :] % M) * (2.0 * np.pi / M)
    hartley = (np.cos(angles) + np.sin(angles)).astype(np.float32)
    window = (np.arange(M // planes)[:, None] * planes + np.arange(8)[None, :]) % M
    depth = hartley[:, window.reshape(-1)]

    def parts(table):
        high = table.astype(ml_dtypes.bfloat16)
        low = (table - high.astype(np.float32)).astype(ml_dtypes.bfloat16)
        return jnp.asarray(np.concatenate([high, high, low], axis=1))

    return (parts(hartley), parts(depth), parts(depth.T))


def stacked_parts(value):
    high = value.astype(jnp.bfloat16)
    low = (value - high.astype(jnp.float32)).astype(jnp.bfloat16)
    return jnp.concatenate([high, low, high], axis=0)


def wave_squares(indices):
    waves = jnp.where(indices < M // 2, indices, indices - M).astype(jnp.float32)
    return waves * waves * ((2.0 * math.pi / M) ** 2)


def mesh_kernel(
    planes,
    params_ref,
    places_ref,
    charges_ref,
    hartley_ref,
    depth_ref,
    back_ref,
    values_ref,
    terms_ref,
    atom_planes,
    atom_columns,
    mesh,
):
    groups, cells, unused, atoms = places_ref.shape
    lanes = 2 * M

    def spread_group(group, carry):
        for cell in range(cells):
            places = places_ref[group, cell]
            fractions = spline_weights(places[3:6])
            bases = places[0:3].astype(jnp.int32)
            window = lax.broadcasted_iota(jnp.int32, (8, atoms), 0)
            along_depth = pick_weight(
                window - (bases[0:1] - group * planes), [w[0:1] for w in fractions]
            )
            index = lax.broadcasted_iota(jnp.int32, (M, atoms), 0)
            along_rows = pick_weight((index - bases[1:2]) & (M - 1), [w[1:2] for w in fractions])
            along_columns = pick_weight(
                (index - bases[2:3]) & (M - 1), [w[2:3] for w in fractions]
            )
            both = jnp.concatenate(
                [stacked_parts(along_rows), stacked_parts(along_columns)], axis=1
            )
            waves = jnp.dot(hartley_ref[...], both, preferred_element_type=jnp.float32)
            row_waves = waves[:, :atoms]
            column_waves = waves[:, atoms:]
            plane_waves = (
                (row_waves[:, None, :] * along_depth[None, :, :])
                .reshape(M * 8, atoms)
                .astype(jnp.bfloat16)
            )
            charges = charges_ref[group, cell]
            terms = jnp.concatenate(
                [column_waves * charges[0:1], column_waves * charges[1:2]], axis=0
            ).astype(jnp.bfloat16)
            atom_planes[group, cell] = plane_waves
            atom_columns[group, cell] = column_waves
            added = lax.dot_general(
                plane_waves, terms, (((1,), (1,)), ((), ())), preferred_element_type=jnp.float32
            )
            mesh[:, pl.ds(pl.multiple_of(group * 8, 8), 8), cell * lanes : (cell + 1) * lanes] = (
                added.reshape(M, 8, lanes)
            )
        return carry

    lax.fori_loop(0, groups, spread_group, 0)

    amplitude = params_ref[0]
    widths = params_ref[1]
    screens = params_ref[2]
    plane_squares = wave_squares(
        lax.broadcasted_iota(jnp.int32, (M, lanes), 0)
    ) + wave_squares(lax.broadcasted_iota(jnp.int32, (M, lanes), 1) & (M - 1))

    def filter_row(row, sums):
        spectrum = jnp.dot(
            depth_ref[...], stacked_parts(mesh[row]), preferred_element_type=jnp.float32
        )
        signed = jnp.where(row < M // 2, row, row - M).astype(jnp.float32)
        squares = plane_squares + signed * signed * ((2.0 * math.pi / M) ** 2)
        screened = 1.0 / (squares + screens)
        gains = (amplitude * (1.0 / M**3)) * jnp.exp((-0.5 * widths) * squares) * screened
        crossed = jnp.zeros((M, lanes), jnp.float32)
        filtered = []
        for cell in range(cells):
            part = spectrum[:, cell * lanes : (cell + 1) * lanes]
            crossed = crossed + part * pltpu.roll(part, M, 1)
            filtered.append(part * gains)
        crossed = crossed * gains
        mesh[row] = jnp.dot(
            back_ref[...],
            stacked_parts(jnp.concatenate(filtered, axis=1)),
            preferred_element_type=jnp.float32,
        )
        pieces = (crossed, crossed * squares, crossed * screened)
        return tuple(
            total + jnp.sum(piece.reshape(M // 8, 8, lanes), axis=0)
            for total, piece in zip(sums, pieces)
        )

    zero = jnp.zeros((8, lanes), jnp.float32)
    sums = lax.fori_loop(0, M, filter_row, (zero, zero, zero))
    for order_index in range(3):
        terms_ref[order_index] = sums[order_index]

    def read_group(group, carry):
        for cell in range(cells):
            window = (
                mesh[
                    :, pl.ds(pl.multiple_of(group * 8, 8), 8), cell * lanes : (cell + 1) * lanes
                ]
                .reshape(M * 8, lanes)
                .astype(jnp.bfloat16)
            )
            inner = lax.dot_general(
                window,
                atom_planes[group, cell],
                (((0,), (0,)), ((), ())),
                preferred_element_type=jnp.float32,
            )
            weighted = inner.reshape(2, M, atoms) * atom_columns[group, cell][None]
            values_ref[group, cell] = jnp.sum(weighted, axis=1)
        return carry

    lax.fori_loop(0, groups, read_group, 0)


def mesh_of_channel(params, places, charges):
    groups, cells, unused, atoms = places.shape
    planes = M // groups
    tables = stacked_tables(planes)
    whole = pl.BlockSpec(memory_space=pltpu.VMEM)
    return pl.pallas_call(
        functools.partial(mesh_kernel, planes),
        out_shape=(
            jax.ShapeDtypeStruct((groups, cells, 2, atoms), jnp.float32),
            jax.ShapeDtypeStruct((3, 8, 2 * M), jnp.float32),
        ),
        in_specs=[pl.BlockSpec(memory_space=pltpu.SMEM)] + [whole] * 5,
        out_specs=(whole, whole),
        scratch_shapes=[
            pltpu.VMEM((groups, cells, M * 8, atoms), jnp.bfloat16),
            pltpu.VMEM((groups, cells, M, atoms), jnp.float32),
            pltpu.VMEM((M, groups * 8, cells * 2 * M), jnp.float32),
        ],
        compiler_params=pltpu.CompilerParams(vmem_limit_bytes=56 * 1024 * 1024),
    )(params, places, charges, *tables)


def by_channel(
    atom_features,
    cotangent,
    charge_weight,
    message_weight,
    amplitude,
    smoothing,
    screening,
    base_cells,
    cell_offsets,
    row_starts,
    block_counts,
):
    cell_count, atom_rows, features = atom_features.shape
    channels = charge_weight.shape[1]
    devices = lax.axis_size("seq")
    blocks = block_counts.shape[1]
    channel = lax.axis_index("seq")
    places = lax.all_gather(
        jnp.concatenate([base_cells.astype(jnp.float32), cell_offsets], axis=1), "seq"
    )
    slot_index = jnp.arange(atom_rows // blocks, dtype=jnp.int32)
    live = (slot_index[None, None, :] < block_counts[:, :, None]).reshape(cell_count, atom_rows)
    live_mask = live.astype(jnp.float32)
    projected = lax.dot_general(
        charge_weight,
        atom_features,
        (((0,), (2,)), ((), ())),
        preferred_element_type=jnp.float32,
    )
    pulled = lax.dot_general(
        message_weight, cotangent, (((1,), (2,)), ((), ())), preferred_element_type=jnp.float32
    )
    charges = (jnp.stack([projected, pulled], axis=2) * live_mask[None, :, None, :]).astype(
        jnp.bfloat16
    )
    own_charges = lax.all_to_all(charges, "seq", split_axis=0, concat_axis=0, tiled=True)
    params = lax.dynamic_slice_in_dim(
        jnp.stack([amplitude, smoothing * smoothing, screening * screening]), channel, 1, 1
    ).reshape(3)
    values, sums = mesh_of_channel(params, places, own_charges.astype(jnp.float32))
    returned = lax.all_to_all(
        values.astype(jnp.bfloat16), "seq", split_axis=0, concat_axis=0, tiled=True
    )
    potential = returned[:, :, 0]
    response = jnp.where(live[None], returned[:, :, 1], jnp.zeros((), jnp.bfloat16))
    outgoing = lax.dot_general(
        potential, message_weight, (((0,), (0,)), ((), ())), preferred_element_type=jnp.float32
    )
    message = (live_mask[:, :, None] * outgoing).astype(jnp.bfloat16)
    atom_gradient = lax.dot_general(
        response, charge_weight, (((0,), (1,)), ((), ())), preferred_element_type=jnp.float32
    ).astype(jnp.bfloat16)
    gradient_scale = 1.0 / math.sqrt(cell_count * atom_rows * devices)
    live_potential = jnp.where(live[None], potential, jnp.zeros((), jnp.bfloat16))
    gradient_in = (
        lax.dot_general(
            atom_features,
            response,
            (((0, 1), (1, 2)), ((), ())),
            preferred_element_type=jnp.float32,
        )
        * gradient_scale
    )
    gradient_out = (
        lax.dot_general(
            live_potential,
            cotangent,
            (((1, 2), (0, 1)), ((), ())),
            preferred_element_type=jnp.float32,
        )
        * gradient_scale
    )
    factors = jnp.stack([jnp.ones((), jnp.float32), -params[1], -2.0 * params[2]])
    own_terms = jnp.sum(sums, axis=(1, 2)) * factors * (0.5 * gradient_scale)
    filter_terms = jnp.where(
        jnp.arange(channels)[None, :] == channel, own_terms[:, None], jnp.zeros((), jnp.float32)
    )
    gradient_in, gradient_out, filter_terms = lax.psum(
        (gradient_in, gradient_out, filter_terms), "seq"
    )
    return (message, atom_gradient, gradient_in, gradient_out, filter_terms)


def solution(mesh):

    def per_device(*arguments):
        by_channels = arguments[2].shape[1] == mesh.shape["seq"]
        return (by_channel if by_channels else on_device)(*arguments)

    in_specs = (
        P("groups", "seq", None),
        P("groups", "seq", None),
        P(),
        P(),
        P(),
        P(),
        P(),
        P("groups", None, "seq"),
        P("groups", None, "seq"),
        P("groups", "seq"),
        P("groups", "seq"),
    )
    out_specs = (
        P("groups", "seq", None),
        P("groups", "seq", None),
        P("groups", None),
        P("groups", None),
        P("groups", None),
    )
    return jax.shard_map(
        per_device, mesh=mesh, in_specs=in_specs, out_specs=out_specs, check_vma=False
    )
```

profile of v0, /device:TPU:0, one launch (start us, length us, event | category | flops | bytes accessed | tf_op | source)
XLA Modules:
  0.0 160.2 jit_solution(15350641561342777304)
XLA Ops:
  0.6 0.0 copy-start
  0.6 0.0 copy-start.7
  0.7 0.7 copy-done.7
  1.4 0.1 broadcast_bitcast_fusion
  1.5 1.3 convolution_bitcast_fusion.1
  2.7 0.0 copy-start.6
  2.7 0.1 copy.46
  2.8 0.0 copy-done
  2.8 0.6 copy-done.6
  3.5 0.2 convolution_bitcast_fusion
  3.7 0.1 copy.47
  3.8 0.8 fusion.4
  4.6 0.0 copy-start.3
  4.6 7.5 %all-to-all-start = ((bf16[16,2,2,512]{3,2,1,0:T(2,128)(2,1)}), bf16[16,2,2,512]{3,2,1,0:T(2,128)(2,1)S(1)}, u32[]{:S(2)}, u32[]{:S(2)}) async-start(bf16[16,2,2,512]{3,2,1,0:T(2,128)(2,1)} %fusion.4), calls=%async_computation | async-start | bytes 131072 | tf_op jit(solution)/shard_map/all_to_all | solution.py:517
  12.1 0.0 copy-done.3
  12.1 0.0 copy-start.4
  12.1 0.7 copy-done.4
  12.8 24.6 %all-gather = f32[32,6,512]{2,1,0:T(8,128)} all-gather(f32[2,6,512]{2,1,0:T(8,128)S(1)} %pad_maximum_fusion), channel_id=2, replica_groups=mesh['groups'=2,'seq'=16] {'seq'}, dimensions={0}, use_global_device_ids=true | all-gather | bytes 417792 | tf_op jit(solution)/shard_map/all_gather | solution.py:499
  37.4 0.0 copy-start.9
  37.4 0.0 copy-start.10
  37.4 0.7 copy-done.9
  38.1 0.0 copy-done.10
  38.1 0.0 copy-start.8
  38.1 0.7 copy-done.8
  38.8 0.7 fusion.18
  39.5 0.5 fusion.21
  41.3 0.0 all-to-all-done
  41.3 0.7 convert_element_type.32.charges_ref
  42.0 44.5 %shard_map.164 = (f32[16,2,2,512]{3,2,1,0:T(2,128)}, f32[3,8,128]{2,1,0:T(8,128)}) custom-call(f32[3]{0:T(128)} %get-tuple-element.12.params_ref, f32[16,2,6,512]{3,2,1,0:T(8,128)} %bitcast.54, f32[16,2,2,512]{3,2,1,0:T(2,128)} %convert_element_type.32.charges_ref, bf16[64,192]{1,0:T(8,128)(2,1)} %constant.30.clone.hartley_ref, ...), custom_call_target="tpu_custom_call" | custom-call | tf_op jit(solution)/shard_map/pallas_call | solution.py:464
  86.5 1.6 convert_element_type.33
  88.0 0.0 copy-start.5
  88.1 3.6 %all-to-all-start.1 = ((bf16[16,2,2,512]{3,2,1,0:T(2,128)(2,1)}), bf16[16,2,2,512]{3,2,1,0:T(2,128)(2,1)S(1)}, u32[]{:S(2)}, u32[]{:S(2)}) async-start(bf16[16,2,2,512]{3,2,1,0:T(2,128)(2,1)} %convert_element_type.33), calls=%async_computation.1 | async-start | bytes 131072 | tf_op jit(solution)/shard_map/all_to_all | solution.py:522
  91.7 0.0 copy-done.5
  91.7 0.1 reduce_sum.9
  91.8 0.1 fusion.14
  91.9 0.1 broadcast_select_fusion
  92.0 6.6 %all-to-all-done.1 = bf16[16,2,2,512]{3,2,1,0:T(2,128)(2,1)S(1)} async-done(((bf16[16,2,2,512]{3,2,1,0:T(2,128)(2,1)}), bf16[16,2,2,512]{3,2,1,0:T(2,128)(2,1)S(1)}, u32[]{:S(2)}, u32[]{:S(2)}) %all-to-all-start.1) | async-done | bytes 65568 | tf_op jit(solution)/shard_map/all_to_all | solution.py:522
  98.6 0.1 fusion.20
  98.7 0.0 copy-start.1
  98.7 1.1 fusion
  99.8 0.2 fusion.1
  100.0 0.0 copy-done.1
  100.0 0.0 copy-start.2
  100.0 0.2 fusion.3
  100.2 0.5 copy-done.2
  100.7 1.1 convolution_convert_fusion
  101.8 58.4 %all-reduce = (f32[256,16]{0,1:T(8,128)}, f32[16,256]{1,0:T(8,128)}, f32[3,16]{1,0:T(4,128)}) all-reduce(f32[256,16]{0,1:T(8,128)S(1)} %fusion.3, f32[16,256]{1,0:T(8,128)S(1)} %fusion.1, f32[3,16]{1,0:T(4,128)S(1)} %broadcast_select_fusion), channel_id=1, replica_groups=mesh['groups'=2,'seq'=16] {'seq'}, use_global_device_ids=true, to_apply=%region_0.1 | all-reduce | flops 8240 | bytes 65920 | tf_op jit(solution)/shard_map/psum | solution.py:559
  (8 shorter events, 0.1 us)
Async XLA Ops:
  0.6 2.2 %copy-start = (bf16[2,512,256]{2,1,0:T(8,128)(2,1)S(1)}, bf16[2,512,256]{2,1,0:T(8,128)(2,1)}, u32[]{:S(2)}) copy-start(bf16[2,512,256]{2,1,0:T(8,128)(2,1)} %param.15) | copy-start | bytes 1572868
  0.6 0.7 copy-start.7
  2.7 0.7 copy-start.6
  4.6 7.5 %copy-start.3 = (s32[2,3,512]{2,0,1:T(2,128)S(1)}, s32[2,3,512]{2,0,1:T(2,128)}, u32[]{:S(2)}) copy-start(s32[2,3,512]{2,0,1:T(2,128)} %param.21) | copy-start | bytes 36868
  4.6 36.7 %all-to-all-start = ((bf16[16,2,2,512]{3,2,1,0:T(2,128)(2,1)}), bf16[16,2,2,512]{3,2,1,0:T(2,128)(2,1)S(1)}, u32[]{:S(2)}, u32[]{:S(2)}) async-start(bf16[16,2,2,512]{3,2,1,0:T(2,128)(2,1)} %fusion.4), calls=%async_computation | async-start | bytes 131072 | tf_op jit(solution)/shard_map/all_to_all | solution.py:517
  12.1 0.7 copy-start.4
  37.4 0.7 copy-start.9
  37.4 0.7 copy-start.10
  38.1 0.7 copy-start.8
  88.0 3.6 %copy-start.5 = (f32[3,8,128]{2,1,0:T(8,128)S(1)}, f32[3,8,128]{2,1,0:T(8,128)}, u32[]{:S(2)}) copy-start(f32[3,8,128]{2,1,0:T(8,128)} %get-tuple-element.8) | copy-start | bytes 36868
  88.1 10.5 %all-to-all-start.1 = ((bf16[16,2,2,512]{3,2,1,0:T(2,128)(2,1)}), bf16[16,2,2,512]{3,2,1,0:T(2,128)(2,1)S(1)}, u32[]{:S(2)}, u32[]{:S(2)}) async-start(bf16[16,2,2,512]{3,2,1,0:T(2,128)(2,1)} %convert_element_type.33), calls=%async_computation.1 | async-start | bytes 131072 | tf_op jit(solution)/shard_map/all_to_all | solution.py:522
  98.7 1.3 copy-start.1
  100.0 0.7 copy-start.2
where the time goes:
time: 161 us; the launch traced here: 160 us
  blocking collectives  83 us (52%)
  Pallas kernels  44.5 us (28%)
  starting transfers between devices  11.2 us (7%)
  waiting for transfers between devices  6.59 us (4%)
  local copies, waits for them, and re-layouts  5.44 us (3%)
  matrix products  4.16 us (3%)
  other arithmetic  3.35 us (2%)
  between operations  2.09 us (1%)
    psum x1, blocking collectives, by_channel(): lax.psum((gradient_in, gradient_out, filter_terms), 'seq')  58.4 us
    pallas_call x1, Pallas kernels, mesh_of_channel(): pl.pallas_call(functools.partial(mesh_kernel, planes), out_shape=(jax.Sha...  44.5 us
    all_gather x1, blocking collectives, by_channel(): lax.all_gather(jnp.concatenate([base_cells.astype(jnp.float32), cell_offs...  24.6 us
    all_to_all x1, starting transfers between devices, by_channel(): lax.all_to_all(charges, 'seq', split_axis=0, concat_axis=0, tiled=True)  7.52 us
    all_to_all x1, waiting for transfers between devices, by_channel(): lax.all_to_all(values.astype(jnp.bfloat16), 'seq', split_axis=0, concat_a...  6.59 us
    unnamed x24, local copies, waits for them, and re-layouts  3.96 us
    all_to_all x1, starting transfers between devices, by_channel(): lax.all_to_all(values.astype(jnp.bfloat16), 'seq', split_axis=0, concat_a...  3.63 us
  transfers between devices with their start and end apart: 2, of which 1 were waited for; matrix products, arithmetic and copies ran while one was open for 1% of the time, Pallas kernels for 0%

commit v1 on v0

--- a/solution.py
+++ b/solution.py
@@ -341,8 +341,7 @@
 def mesh_kernel(
     planes,
     params_ref,
-    places_ref,
-    charges_ref,
+    atoms_ref,
     hartley_ref,
     depth_ref,
     back_ref,
@@ -352,12 +351,12 @@
     atom_columns,
     mesh,
 ):
-    groups, cells, unused, atoms = places_ref.shape
+    groups, cells, unused, atoms = atoms_ref.shape
     lanes = 2 * M
 
     def spread_group(group, carry):
         for cell in range(cells):
-            places = places_ref[group, cell]
+            places = atoms_ref[group, cell]
             fractions = spline_weights(places[3:6])
             bases = places[0:3].astype(jnp.int32)
             window = lax.broadcasted_iota(jnp.int32, (8, atoms), 0)
@@ -380,9 +379,8 @@
                 .reshape(M * 8, atoms)
                 .astype(jnp.bfloat16)
             )
-            charges = charges_ref[group, cell]
             terms = jnp.concatenate(
-                [column_waves * charges[0:1], column_waves * charges[1:2]], axis=0
+                [column_waves * places[6:7], column_waves * places[7:8]], axis=0
             ).astype(jnp.bfloat16)
             atom_planes[group, cell] = plane_waves
             atom_columns[group, cell] = column_waves
@@ -456,8 +454,8 @@
     lax.fori_loop(0, groups, read_group, 0)
 
 
-def mesh_of_channel(params, places, charges):
-    groups, cells, unused, atoms = places.shape
+def mesh_of_channel(params, atom_blocks):
+    groups, cells, unused, atoms = atom_blocks.shape
     planes = M // groups
     tables = stacked_tables(planes)
     whole = pl.BlockSpec(memory_space=pltpu.VMEM)
@@ -467,7 +465,7 @@
             jax.ShapeDtypeStruct((groups, cells, 2, atoms), jnp.float32),
             jax.ShapeDtypeStruct((3, 8, 2 * M), jnp.float32),
         ),
-        in_specs=[pl.BlockSpec(memory_space=pltpu.SMEM)] + [whole] * 5,
+        in_specs=[pl.BlockSpec(memory_space=pltpu.SMEM)] + [whole] * 4,
         out_specs=(whole, whole),
         scratch_shapes=[
             pltpu.VMEM((groups, cells, M * 8, atoms), jnp.bfloat16),
@@ -475,7 +473,131 @@
             pltpu.VMEM((M, groups * 8, cells * 2 * M), jnp.float32),
         ],
         compiler_params=pltpu.CompilerParams(vmem_limit_bytes=56 * 1024 * 1024),
-    )(params, places, charges, *tables)
+    )(params, atom_blocks, *tables)
+
+
+def to_peer(source, target, send_sems, receive_sems, peer, sender):
+    return pltpu.make_async_remote_copy(
+        src_ref=source,
+        dst_ref=target,
+        send_sem=send_sems.at[peer],
+        recv_sem=receive_sems.at[sender],
+        device_id={"seq": peer},
+        device_id_type=pl.DeviceIdType.MESH,
+    )
+
+
+def greet_peers(count, own):
+    barrier = pltpu.get_barrier_semaphore()
+
+    def greet(step, carry):
+        pl.semaphore_signal(
+            barrier,
+            inc=1,
+            device_id={"seq": lax.rem(own + step, count)},
+            device_id_type=pl.DeviceIdType.MESH,
+        )
+        return carry
+
+    lax.fori_loop(1, count, greet, 0)
+    pl.semaphore_wait(barrier, count - 1)
+
+
+def exchange_kernel(count, given_ref, taken_ref, send_sems, receive_sems):
+    own = lax.axis_index("seq")
+    greet_peers(count, own)
+
+    def send(step, carry):
+        peer = lax.rem(own + step, count)
+        to_peer(
+            given_ref.at[peer], taken_ref.at[own], send_sems, receive_sems, peer, own
+        ).start()
+        return carry
+
+    lax.fori_loop(1, count, send, 0)
+    taken_ref[own] = given_ref[own]
+
+    def finish(step, carry):
+        peer = lax.rem(own + step, count)
+        copy = to_peer(
+            given_ref.at[peer], taken_ref.at[peer], send_sems, receive_sems, peer, peer
+        )
+        copy.wait_send()
+        copy.wait_recv()
+        return carry
+
+    lax.fori_loop(1, count, finish, 0)
+
+
+def exchanged(blocks, collective_id):
+    count = blocks.shape[0]
+    whole = pl.BlockSpec(memory_space=pltpu.VMEM)
+    return pl.pallas_call(
+        functools.partial(exchange_kernel, count),
+        out_shape=jax.ShapeDtypeStruct(blocks.shape, blocks.dtype),
+        in_specs=[whole],
+        out_specs=whole,
+        scratch_shapes=[
+            pltpu.SemaphoreType.DMA((count,)),
+            pltpu.SemaphoreType.DMA((count,)),
+        ],
+        compiler_params=pltpu.CompilerParams(collective_id=collective_id, has_side_effects=True),
+    )(blocks)
+
+
+def total_kernel(
+    count, given_ref, fixed_ref, totals_ref, landed, send_sems, receive_sems, spread_sems, total_sems
+):
+    own = lax.axis_index("seq")
+    greet_peers(count, own)
+
+    def send(step, carry):
+        peer = lax.rem(own + step, count)
+        to_peer(given_ref.at[peer], landed.at[own], send_sems, receive_sems, peer, own).start()
+        return carry
+
+    lax.fori_loop(1, count, send, 0)
+
+    def gather(step, total):
+        peer = lax.rem(own + step, count)
+        copy = to_peer(given_ref.at[peer], landed.at[peer], send_sems, receive_sems, peer, peer)
+        copy.wait_send()
+        copy.wait_recv()
+        return total + landed[peer]
+
+    totals_ref[own] = lax.fori_loop(1, count, gather, given_ref[own] + fixed_ref[...])
+
+    def spread(step, carry):
+        peer = lax.rem(own + step, count)
+        to_peer(totals_ref.at[own], totals_ref.at[own], spread_sems, total_sems, peer, own).start()
+        return carry
+
+    lax.fori_loop(1, count, spread, 0)
+
+    def finish(step, carry):
+        peer = lax.rem(own + step, count)
+        copy = to_peer(
+            totals_ref.at[own], totals_ref.at[peer], spread_sems, total_sems, peer, peer
+        )
+        copy.wait_send()
+        copy.wait_recv()
+        return carry
+
+    lax.fori_loop(1, count, finish, 0)
+
+
+def totals_of_channels(blocks, fixed, collective_id):
+    count = blocks.shape[0]
+    whole = pl.BlockSpec(memory_space=pltpu.VMEM)
+    sems = pltpu.SemaphoreType.DMA((count,))
+    return pl.pallas_call(
+        functools.partial(total_kernel, count),
+        out_shape=jax.ShapeDtypeStruct(blocks.shape, blocks.dtype),
+        in_specs=[whole, whole],
+        out_specs=whole,
+        scratch_shapes=[pltpu.VMEM(blocks.shape, blocks.dtype), sems, sems, sems, sems],
+        compiler_params=pltpu.CompilerParams(collective_id=collective_id, has_side_effects=True),
+    )(blocks, fixed)
 
 
 def by_channel(
@@ -496,9 +618,6 @@
     devices = lax.axis_size("seq")
     blocks = block_counts.shape[1]
     channel = lax.axis_index("seq")
-    places = lax.all_gather(
-        jnp.concatenate([base_cells.astype(jnp.float32), cell_offsets], axis=1), "seq"
-    )
     slot_index = jnp.arange(atom_rows // blocks, dtype=jnp.int32)
     live = (slot_index[None, None, :] < block_counts[:, :, None]).reshape(cell_count, atom_rows)
     live_mask = live.astype(jnp.float32)
@@ -514,14 +633,20 @@
     charges = (jnp.stack([projected, pulled], axis=2) * live_mask[None, :, None, :]).astype(
         jnp.bfloat16
     )
-    own_charges = lax.all_to_all(charges, "seq", split_axis=0, concat_axis=0, tiled=True)
+    places = jnp.concatenate([base_cells.astype(jnp.float32), cell_offsets], axis=1)
+    blocks_out = jnp.concatenate(
+        [
+            jnp.broadcast_to(places[None], (devices,) + places.shape),
+            charges.astype(jnp.float32),
+        ],
+        axis=2,
+    )
+    atoms_in = exchanged(blocks_out, 0)
     params = lax.dynamic_slice_in_dim(
         jnp.stack([amplitude, smoothing * smoothing, screening * screening]), channel, 1, 1
     ).reshape(3)
-    values, sums = mesh_of_channel(params, places, own_charges.astype(jnp.float32))
-    returned = lax.all_to_all(
-        values.astype(jnp.bfloat16), "seq", split_axis=0, concat_axis=0, tiled=True
-    )
+    values, sums = mesh_of_channel(params, atoms_in)
+    returned = exchanged(values, 1).astype(jnp.bfloat16)
     potential = returned[:, :, 0]
     response = jnp.where(live[None], returned[:, :, 1], jnp.zeros((), jnp.bfloat16))
     outgoing = lax.dot_general(
@@ -533,32 +658,36 @@
     ).astype(jnp.bfloat16)
     gradient_scale = 1.0 / math.sqrt(cell_count * atom_rows * devices)
     live_potential = jnp.where(live[None], potential, jnp.zeros((), jnp.bfloat16))
-    gradient_in = (
-        lax.dot_general(
-            atom_features,
-            response,
-            (((0, 1), (1, 2)), ((), ())),
-            preferred_element_type=jnp.float32,
-        )
-        * gradient_scale
-    )
-    gradient_out = (
-        lax.dot_general(
-            live_potential,
-            cotangent,
-            (((1, 2), (0, 1)), ((), ())),
-            preferred_element_type=jnp.float32,
-        )
-        * gradient_scale
+    gradient_in = lax.dot_general(
+        response,
+        atom_features,
+        (((1, 2), (0, 1)), ((), ())),
+        preferred_element_type=jnp.float32,
+    )
+    gradient_out = lax.dot_general(
+        live_potential,
+        cotangent,
+        (((1, 2), (0, 1)), ((), ())),
+        preferred_element_type=jnp.float32,
     )
     factors = jnp.stack([jnp.ones((), jnp.float32), -params[1], -2.0 * params[2]])
-    own_terms = jnp.sum(sums, axis=(1, 2)) * factors * (0.5 * gradient_scale)
-    filter_terms = jnp.where(
-        jnp.arange(channels)[None, :] == channel, own_terms[:, None], jnp.zeros((), jnp.float32)
-    )
-    gradient_in, gradient_out, filter_terms = lax.psum(
-        (gradient_in, gradient_out, filter_terms), "seq"
-    )
+    own_terms = jnp.sum(sums, axis=(1, 2)) * factors * 0.5
+    width = 128
+    rows = features // width
+    padding = 8 - 2 * rows
+    blocks_out = jnp.concatenate(
+        [
+            gradient_in.reshape(channels, rows, width),
+            gradient_out.reshape(channels, rows, width),
+            jnp.zeros((channels, padding, width), jnp.float32),
+        ],
+        axis=1,
+    )
+    fixed = jnp.pad(own_terms[None, :], ((2 * rows, padding - 1), (0, width - 3)))
+    totals = totals_of_channels(blocks_out, fixed, 2) * gradient_scale
+    gradient_in = totals[:, :rows].reshape(channels, features).T
+    gradient_out = totals[:, rows : 2 * rows].reshape(channels, features)
+    filter_terms = totals[:, 2 * rows, :3].T
     return (message, atom_gradient, gradient_in, gradient_out, filter_terms)
 
 

time: 161 us -> 107 us (0.66)
  blocking collectives: 83 us -> 0 us
  Pallas kernels: 44.5 us -> 88.3 us
  starting transfers between devices: 11.2 us -> 0 us
  waiting for transfers between devices: 6.59 us -> 0 us
  other arithmetic: 3.35 us -> 6.78 us
    psum x1 -> x0, blocking collectives: 58.4 us -> none  [by_channel(): lax.psum((gradient_in, gradient_out, filter_terms), 'seq')]
    pallas_call x0 -> x3, Pallas kernels: none -> 44.1 us  [the longest x2 28.7 us: exchanged(): pl.pallas_call(functools.partial(exchange_kernel, count), out_shape=jax.S...]
    all_gather x1 -> x0, blocking collectives: 24.6 us -> none  [by_channel(): lax.all_gather(jnp.concatenate([base_cells.astype(jnp.float32), cell_offs...]
    all_to_all x2 -> x0, starting transfers between devices: 11.2 us -> none  [the longest x1 7.52 us: by_channel(): lax.all_to_all(charges, 'seq', split_axis=0, concat_axis=0, tiled=True)]
    all_to_all x2 -> x0, waiting for transfers between devices: 6.59 us -> none  [the longest x1 6.59 us: by_channel(): lax.all_to_all(values.astype(jnp.bfloat16), 'seq', split_axis=0, concat_a...]
    convert_element_type x3 -> x2, other arithmetic: 3.04 us -> 1.08 us  [the longest x1 0.96 us: by_channel(): returned = exchanged(values, 1).astype(jnp.bfloat16)]
    unnamed x24 -> x13, local copies, waits for them, and re-layouts: 3.96 us -> 2.6 us
  transfers between devices with their start and end apart: 2 -> 0, of which waited for: 1 -> 0; matrix products, arithmetic and copies ran while one was open for 1% -> 0% of each run, Pallas kernels for 0% -> 0%
where the time goes in v1:
time: 107 us; the launch traced here: 106 us
  Pallas kernels  88.3 us (83%)
  other arithmetic  6.78 us (6%)
  local copies, waits for them, and re-layouts  5.43 us (5%)
  matrix products  3.79 us (4%)
  between operations  2.11 us (2%)
    pallas_call x1, Pallas kernels, mesh_of_channel(): pl.pallas_call(functools.partial(mesh_kernel, planes), out_shape=(jax.Sha...  44.2 us
    pallas_call x2, Pallas kernels, exchanged(): pl.pallas_call(functools.partial(exchange_kernel, count), out_shape=jax.S...  28.7 us
    pallas_call x1, Pallas kernels, totals_of_channels(): pl.pallas_call(functools.partial(total_kernel, count), out_shape=jax.Shap...  15.4 us
    unnamed x13, local copies, waits for them, and re-layouts  2.6 us

profile of v1, /device:TPU:0, one launch (start us, length us, event | category | flops | bytes accessed | tf_op | source)
XLA Modules:
  0.0 106.4 jit_solution(2988743343466796060)
XLA Ops:
  0.6 0.0 copy-start
  0.6 0.0 copy-start.1
  0.7 0.1 pad.10.clone
  0.7 0.7 multiply_bitcast_fusion
  1.5 0.7 pad_maximum_fusion.2
  2.2 0.7 fusion.22
  2.9 0.5 fusion.25
  4.7 0.8 broadcast_bitcast_fusion
  5.4 0.7 convert_element_type.32
  6.2 0.7 pad_maximum_fusion.1
  6.9 0.0 copy-done
  6.9 0.9 convolution_bitcast_fusion.1
  7.8 0.0 copy-start.4
  7.8 0.1 copy.44
  7.9 0.0 copy-done.1
  7.9 0.6 copy-done.4
  8.6 0.2 convolution_bitcast_fusion
  8.8 0.1 copy.45
  8.9 0.1 fusion.6
  9.0 0.1 broadcast_in_dim.34
  9.1 0.9 pad_maximum_fusion.given_ref
  10.0 17.1 %shard_map.164.atoms_ref = f32[16,2,8,512]{3,2,1,0:T(8,128)} custom-call(f32[16,2,8,512]{3,2,1,0:T(8,128)} %pad_maximum_fusion.given_ref), custom_call_target="tpu_custom_call" | custom-call | tf_op jit(solution)/shard_map/pallas_call | solution.py:535
  27.1 44.2 %shard_map.165 = (f32[16,2,2,512]{3,2,1,0:T(2,128)}, f32[3,8,128]{2,1,0:T(8,128)}) custom-call(f32[3]{0:T(128)} %get-tuple-element.9.params_ref, f32[16,2,8,512]{3,2,1,0:T(8,128)} %shard_map.164.atoms_ref, bf16[64,192]{1,0:T(8,128)(2,1)} %constant.30.clone.hartley_ref, bf16[64,384]{1,0:T(8,128)(2,1)} %constant.31.clone.depth_ref, ...), custom_call_target="tpu_custom_call" | custom-call | tf_op jit(solution)/shard_map/pallas_call | solution.py:462
  71.3 11.6 %shard_map.166 = f32[16,2,2,512]{3,2,1,0:T(2,128)} custom-call(f32[16,2,2,512]{3,2,1,0:T(2,128)} %get-tuple-element.7.given_ref), custom_call_target="tpu_custom_call" | custom-call | tf_op jit(solution)/shard_map/pallas_call | solution.py:535
  82.9 0.0 copy-start.3
  82.9 1.0 convert_element_type.35
  83.9 0.0 copy-done.3
  83.9 0.1 reduce_sum.11
  84.0 0.1 fusion.20
  84.1 0.6 pad.4.fixed_ref
  84.7 0.2 broadcast_select_fusion.1
  84.9 0.2 convolution_bitcast_fusion.3
  85.1 0.2 convolution_bitcast_fusion.2
  85.3 0.7 maximum_maximum_fusion.given_ref
  86.0 15.4 %shard_map.167 = f32[16,8,128]{2,1,0:T(8,128)} custom-call(f32[16,8,128]{2,1,0:T(8,128)} %maximum_maximum_fusion.given_ref, f32[8,128]{1,0:T(8,128)} %pad.4.fixed_ref), custom_call_target="tpu_custom_call" | custom-call | tf_op jit(solution)/shard_map/pallas_call | solution.py:593
  101.4 0.8 broadcast_multiply_fusion
  102.3 0.7 copy.41
  102.9 0.6 copy.79
  103.5 0.6 copy.80
  104.1 0.0 copy-start.2
  104.1 1.1 %fusion = bf16[2,512,256]{2,1,0:T(8,128)(2,1)} fusion(f32[2,512]{1,0:T(2,128)S(1)} %get-tuple-element.11, bf16[16,2,1,512]{3,2,1,0:T(2,128)(2,1)S(1)} %get-tuple-element.18, bf16[16,256]{1,0:T(8,128)(2,1)S(1)} %copy-done.4), kind=kOutput, calls=%fused_computation.1 | convolution fusion | flops 8912896 | bytes 569344 | tf_op jit(solution)/shard_map/dot_general | solution.py:652
  105.3 0.0 copy-done.2
  105.3 1.1 %convolution_convert_fusion = bf16[2,512,256]{2,1,0:T(8,128)(2,1)} fusion(bf16[16,2,1,512]{3,2,1,0:T(2,128)(2,1)S(1)} %get-tuple-element.17, pred[2,512]{1,0:T(4,128)(4,1)S(1)} %get-tuple-element.12, bf16[256,16]{0,1:T(8,128)(2,1)S(1)} %copy-done.2), kind=kOutput, calls=%fused_computation.2 | convolution fusion | flops 8667136 | bytes 566272 | tf_op jit(solution)/shard_map/dot_general | solution.py:656
  (8 shorter events, 0.1 us)
Async XLA Ops:
  0.6 6.3 %copy-start = (bf16[2,512,256]{2,1,0:T(8,128)(2,1)S(1)}, bf16[2,512,256]{2,1,0:T(8,128)(2,1)}, u32[]{:S(2)}) copy-start(bf16[2,512,256]{2,1,0:T(8,128)(2,1)} %param.14) | copy-start | bytes 1572868
  0.6 7.3 %copy-start.1 = (bf16[2,512,256]{2,1,0:T(8,128)(2,1)S(1)}, bf16[2,512,256]{2,1,0:T(8,128)(2,1)}, u32[]{:S(2)}) copy-start(bf16[2,512,256]{2,1,0:T(8,128)(2,1)} %param.15) | copy-start | bytes 1572868
  7.8 0.7 copy-start.4
  82.9 1.0 copy-start.3
  104.1 1.1 %copy-start.2 = (bf16[256,16]{0,1:T(8,128)(2,1)S(1)}, bf16[256,16]{0,1:T(8,128)(2,1)}, u32[]{:S(2)}) copy-start(bf16[256,16]{0,1:T(8,128)(2,1)} %param.16) | copy-start | bytes 24580

commit v2 on v1

--- a/solution.py
+++ b/solution.py
@@ -341,20 +341,47 @@
 def mesh_kernel(
     planes,
     params_ref,
-    atoms_ref,
+    given_ref,
     hartley_ref,
     depth_ref,
     back_ref,
+    returned_ref,
+    terms_ref,
+    atoms_ref,
     values_ref,
-    terms_ref,
     atom_planes,
     atom_columns,
     mesh,
+    plane_gains,
+    send_sems,
+    receive_sems,
+    back_sems,
+    return_sems,
 ):
-    groups, cells, unused, atoms = atoms_ref.shape
+    groups, cells, unused, atoms = given_ref.shape
     lanes = 2 * M
-
-    def spread_group(group, carry):
+    own = lax.axis_index("seq")
+    greet_peers(groups, own)
+
+    def send_atoms(step, carry):
+        peer = lax.rem(own + step, groups)
+        to_peer(
+            given_ref.at[peer], atoms_ref.at[own], send_sems, receive_sems, peer, own
+        ).start()
+        return carry
+
+    lax.fori_loop(1, groups, send_atoms, 0)
+    atoms_ref[own] = given_ref[own]
+
+    def spread_group(step, carry):
+        group = lax.rem(own + groups - step, groups)
+
+        @pl.when(step > 0)
+        def arrive():
+            to_peer(
+                given_ref.at[group], atoms_ref.at[group], send_sems, receive_sems, group, group
+            ).wait_recv()
+
         for cell in range(cells):
             places = atoms_ref[group, cell]
             fractions = spline_weights(places[3:6])
@@ -400,15 +427,18 @@
     plane_squares = wave_squares(
         lax.broadcasted_iota(jnp.int32, (M, lanes), 0)
     ) + wave_squares(lax.broadcasted_iota(jnp.int32, (M, lanes), 1) & (M - 1))
+    plane_gains[...] = (amplitude * (1.0 / M**3)) * jnp.exp((-0.5 * widths) * plane_squares)
 
     def filter_row(row, sums):
         spectrum = jnp.dot(
             depth_ref[...], stacked_parts(mesh[row]), preferred_element_type=jnp.float32
         )
         signed = jnp.where(row < M // 2, row, row - M).astype(jnp.float32)
-        squares = plane_squares + signed * signed * ((2.0 * math.pi / M) ** 2)
+        row_square = signed * signed * ((2.0 * math.pi / M) ** 2)
+        squares = plane_squares + row_square
         screened = 1.0 / (squares + screens)
-        gains = (amplitude * (1.0 / M**3)) * jnp.exp((-0.5 * widths) * squares) * screened
+        row_gain = jnp.exp(jnp.full((1, lanes), (-0.5 * widths) * row_square, jnp.float32))
+        gains = plane_gains[...] * row_gain * screened
         crossed = jnp.zeros((M, lanes), jnp.float32)
         filtered = []
         for cell in range(cells):
@@ -428,11 +458,12 @@
         )
 
     zero = jnp.zeros((8, lanes), jnp.float32)
-    sums = lax.fori_loop(0, M, filter_row, (zero, zero, zero))
+    sums = lax.fori_loop(0, M, filter_row, (zero, zero, zero), unroll=4)
     for order_index in range(3):
         terms_ref[order_index] = sums[order_index]
 
-    def read_group(group, carry):
+    def read_group(step, carry):
+        group = lax.rem(own + step, groups)
         for cell in range(cells):
             window = (
                 mesh[
@@ -449,15 +480,38 @@
             )
             weighted = inner.reshape(2, M, atoms) * atom_columns[group, cell][None]
             values_ref[group, cell] = jnp.sum(weighted, axis=1)
+
+        @pl.when(step < groups)
+        def give_back():
+            to_peer(
+                values_ref.at[group], returned_ref.at[own], back_sems, return_sems, group, own
+            ).start()
+
         return carry
 
-    lax.fori_loop(0, groups, read_group, 0)
+    lax.fori_loop(1, groups + 1, read_group, 0)
+    returned_ref[own] = values_ref[own]
+
+    def finish(step, carry):
+        peer = lax.rem(own + groups - step, groups)
+        to_peer(
+            given_ref.at[peer], atoms_ref.at[peer], send_sems, receive_sems, peer, peer
+        ).wait_send()
+        copy = to_peer(
+            values_ref.at[peer], returned_ref.at[peer], back_sems, return_sems, peer, peer
+        )
+        copy.wait_send()
+        copy.wait_recv()
+        return carry
+
+    lax.fori_loop(1, groups, finish, 0)
 
 
 def mesh_of_channel(params, atom_blocks):
     groups, cells, unused, atoms = atom_blocks.shape
     planes = M // groups
     tables = stacked_tables(planes)
+    sems = pltpu.SemaphoreType.DMA((groups,))
     whole = pl.BlockSpec(memory_space=pltpu.VMEM)
     return pl.pallas_call(
         functools.partial(mesh_kernel, planes),
@@ -468,11 +522,20 @@
         in_specs=[pl.BlockSpec(memory_space=pltpu.SMEM)] + [whole] * 4,
         out_specs=(whole, whole),
         scratch_shapes=[
+            pltpu.VMEM(atom_blocks.shape, jnp.float32),
+            pltpu.VMEM((groups, cells, 2, atoms), jnp.float32),
             pltpu.VMEM((groups, cells, M * 8, atoms), jnp.bfloat16),
             pltpu.VMEM((groups, cells, M, atoms), jnp.float32),
             pltpu.VMEM((M, groups * 8, cells * 2 * M), jnp.float32),
+            pltpu.VMEM((M, 2 * M), jnp.float32),
+            sems,
+            sems,
+            sems,
+            sems,
         ],
-        compiler_params=pltpu.CompilerParams(vmem_limit_bytes=56 * 1024 * 1024),
+        compiler_params=pltpu.CompilerParams(
+            collective_id=0, has_side_effects=True, vmem_limit_bytes=56 * 1024 * 1024
+        ),
     )(params, atom_blocks, *tables)
 
 
@@ -501,48 +564,6 @@
 
     lax.fori_loop(1, count, greet, 0)
     pl.semaphore_wait(barrier, count - 1)
-
-
-def exchange_kernel(count, given_ref, taken_ref, send_sems, receive_sems):
-    own = lax.axis_index("seq")
-    greet_peers(count, own)
-
-    def send(step, carry):
-        peer = lax.rem(own + step, count)
-        to_peer(
-            given_ref.at[peer], taken_ref.at[own], send_sems, receive_sems, peer, own
-        ).start()
-        return carry
-
-    lax.fori_loop(1, count, send, 0)
-    taken_ref[own] = given_ref[own]
-
-    def finish(step, carry):
-        peer = lax.rem(own + step, count)
-        copy = to_peer(
-            given_ref.at[peer], taken_ref.at[peer], send_sems, receive_sems, peer, peer
-        )
-        copy.wait_send()
-        copy.wait_recv()
-        return carry
-
-    lax.fori_loop(1, count, finish, 0)
-
-
-def exchanged(blocks, collective_id):
-    count = blocks.shape[0]
-    whole = pl.BlockSpec(memory_space=pltpu.VMEM)
-    return pl.pallas_call(
-        functools.partial(exchange_kernel, count),
-        out_shape=jax.ShapeDtypeStruct(blocks.shape, blocks.dtype),
-        in_specs=[whole],
-        out_specs=whole,
-        scratch_shapes=[
-            pltpu.SemaphoreType.DMA((count,)),
-            pltpu.SemaphoreType.DMA((count,)),
-        ],
-        compiler_params=pltpu.CompilerParams(collective_id=collective_id, has_side_effects=True),
-    )(blocks)
 
 
 def total_kernel(
@@ -641,12 +662,11 @@
         ],
         axis=2,
     )
-    atoms_in = exchanged(blocks_out, 0)
     params = lax.dynamic_slice_in_dim(
         jnp.stack([amplitude, smoothing * smoothing, screening * screening]), channel, 1, 1
     ).reshape(3)
-    values, sums = mesh_of_channel(params, atoms_in)
-    returned = exchanged(values, 1).astype(jnp.bfloat16)
+    returned, sums = mesh_of_channel(params, blocks_out)
+    returned = returned.astype(jnp.bfloat16)
     potential = returned[:, :, 0]
     response = jnp.where(live[None], returned[:, :, 1], jnp.zeros((), jnp.bfloat16))
     outgoing = lax.dot_general(
@@ -684,7 +704,7 @@
         axis=1,
     )
     fixed = jnp.pad(own_terms[None, :], ((2 * rows, padding - 1), (0, width - 3)))
-    totals = totals_of_channels(blocks_out, fixed, 2) * gradient_scale
+    totals = totals_of_channels(blocks_out, fixed, 1) * gradient_scale
     gradient_in = totals[:, :rows].reshape(channels, features).T
     gradient_out = totals[:, rows : 2 * rows].reshape(channels, features)
     filter_terms = totals[:, 2 * rows, :3].T

time: 107 us -> 83.4 us (0.78)
  Pallas kernels: 88.3 us -> 64.8 us
    pallas_call x2 -> x0, Pallas kernels: 28.7 us -> none  [exchanged(): pl.pallas_call(functools.partial(exchange_kernel, count), out_shape=jax.S...]
    pallas_call x1, Pallas kernels: 44.2 us -> 49.5 us  [mesh_of_channel(): pl.pallas_call(functools.partial(mesh_kernel, planes), out_shape=(jax.Sha...]
where the time goes in v2:
time: 83.4 us; the launch traced here: 82.9 us
  Pallas kernels  64.8 us (78%)
  other arithmetic  6.78 us (8%)
  local copies, waits for them, and re-layouts  5.43 us (7%)
  matrix products  3.79 us (5%)
  between operations  2.1 us (3%)
    pallas_call x1, Pallas kernels, mesh_of_channel(): pl.pallas_call(functools.partial(mesh_kernel, planes), out_shape=(jax.Sha...  49.5 us
    pallas_call x1, Pallas kernels, totals_of_channels(): pl.pallas_call(functools.partial(total_kernel, count), out_shape=jax.Shap...  15.3 us
    unnamed x13, local copies, waits for them, and re-layouts  2.6 us

profile of v2, /device:TPU:0, one launch (start us, length us, event | category | flops | bytes accessed | tf_op | source)
XLA Modules:
  0.0 82.9 jit_solution(12922553690334257479)
XLA Ops:
  0.6 0.0 copy-start
  0.6 0.0 copy-start.1
  0.7 0.1 pad.10.clone
  0.7 0.7 multiply_bitcast_fusion
  1.5 0.7 pad_maximum_fusion.2
  2.2 0.7 fusion.22
  2.9 0.5 fusion.25
  4.7 0.8 broadcast_bitcast_fusion
  5.4 0.7 convert_element_type.32
  6.2 0.7 pad_maximum_fusion.1
  6.9 0.0 copy-done
  6.9 0.9 %convolution_bitcast_fusion.1 = f32[16,2,1,512]{3,0,1,2:T(8,128)S(1)} fusion(bf16[2,512,256]{2,1,0:T(8,128)(2,1)S(1)} %copy-done, bf16[256,16]{0,1:T(8,128)(2,1)} %param.16), kind=kOutput, calls=%fused_computation.4 | convolution fusion | flops 8388608 | bytes 598016 | tf_op jit(solution)/shard_map/dot_general | solution.py:645
  7.8 0.0 copy-start.4
  7.8 0.1 copy.44
  7.9 0.0 copy-done.1
  7.9 0.6 copy-done.4
  8.6 0.2 convolution_bitcast_fusion
  8.8 0.1 copy.45
  8.9 0.1 fusion.6
  9.0 0.1 broadcast_in_dim.34
  9.1 0.9 %pad_maximum_fusion.given_ref = f32[16,2,8,512]{3,2,1,0:T(8,128)} fusion(f32[16,2,2,512]{3,2,1,0:T(2,128)S(1)} %fusion.6, f32[16,2,6,512]{3,2,1,0:T(8,128)S(1)} %broadcast_in_dim.34), kind=kLoop, calls=%fused_computation.11 | loop fusion | flops 131072 | bytes 1048576 | tf_op jit(solution)/shard_map/concatenate | solution.py:658
  10.0 49.5 %shard_map.164 = (f32[16,2,2,512]{3,2,1,0:T(2,128)}, f32[3,8,128]{2,1,0:T(8,128)}) custom-call(f32[3]{0:T(128)} %get-tuple-element.9.params_ref, f32[16,2,8,512]{3,2,1,0:T(8,128)} %pad_maximum_fusion.given_ref, bf16[64,192]{1,0:T(8,128)(2,1)} %constant.30.clone.hartley_ref, bf16[64,384]{1,0:T(8,128)(2,1)} %constant.31.clone.depth_ref, ...), custom_call_target="tpu_custom_call" | custom-call | tf_op jit(solution)/shard_map/pallas_call | solution.py:516
  59.5 0.0 copy-start.3
  59.5 1.0 %convert_element_type.35 = bf16[16,2,2,512]{3,2,1,0:T(2,128)(2,1)S(1)} convert(f32[16,2,2,512]{3,2,1,0:T(2,128)} %get-tuple-element.7) | non-fusion elementwise | flops 32768 | bytes 196608 | tf_op jit(solution)/shard_map/convert_element_type | solution.py:669
  60.4 0.0 copy-done.3
  60.5 0.1 reduce_sum.11
  60.6 0.1 fusion.20
  60.6 0.6 pad.4.fixed_ref
  61.2 0.2 broadcast_select_fusion.1
  61.5 0.2 convolution_bitcast_fusion.3
  61.7 0.2 convolution_bitcast_fusion.2
  61.9 0.7 maximum_maximum_fusion.given_ref
  62.6 15.3 %shard_map.165 = f32[16,8,128]{2,1,0:T(8,128)} custom-call(f32[16,8,128]{2,1,0:T(8,128)} %maximum_maximum_fusion.given_ref, f32[8,128]{1,0:T(8,128)} %pad.4.fixed_ref), custom_call_target="tpu_custom_call" | custom-call | tf_op jit(solution)/shard_map/pallas_call | solution.py:614
  77.9 0.8 %broadcast_multiply_fusion = f32[16,8,128]{2,1,0:T(8,128)S(1)} fusion(f32[16,8,128]{2,1,0:T(8,128)} %shard_map.165), kind=kLoop, calls=%fused_computation.26 | loop fusion | flops 16384 | bytes 131072 | tf_op jit(solution)/shard_map/mul | solution.py:707
  78.8 0.7 copy.41
  79.4 0.6 copy.79
  80.0 0.6 copy.80
  80.7 0.0 copy-start.2
  80.7 1.1 %fusion = bf16[2,512,256]{2,1,0:T(8,128)(2,1)} fusion(f32[2,512]{1,0:T(2,128)S(1)} %get-tuple-element.11, bf16[16,2,1,512]{3,2,1,0:T(2,128)(2,1)S(1)} %get-tuple-element.18, bf16[16,256]{1,0:T(8,128)(2,1)S(1)} %copy-done.4), kind=kOutput, calls=%fused_computation.1 | convolution fusion | flops 8912896 | bytes 569344 | tf_op jit(solution)/shard_map/dot_general | solution.py:672
  81.8 0.0 copy-done.2
  81.8 1.1 %convolution_convert_fusion = bf16[2,512,256]{2,1,0:T(8,128)(2,1)} fusion(bf16[16,2,1,512]{3,2,1,0:T(2,128)(2,1)S(1)} %get-tuple-element.17, pred[2,512]{1,0:T(4,128)(4,1)S(1)} %get-tuple-element.12, bf16[256,16]{0,1:T(8,128)(2,1)S(1)} %copy-done.2), kind=kOutput, calls=%fused_computation.2 | convolution fusion | flops 8667136 | bytes 566272 | tf_op jit(solution)/shard_map/dot_general | solution.py:676
  (8 shorter events, 0.1 us)
Async XLA Ops:
  0.6 6.3 %copy-start = (bf16[2,512,256]{2,1,0:T(8,128)(2,1)S(1)}, bf16[2,512,256]{2,1,0:T(8,128)(2,1)}, u32[]{:S(2)}) copy-start(bf16[2,512,256]{2,1,0:T(8,128)(2,1)} %param.14) | copy-start | bytes 1572868
  0.6 7.3 %copy-start.1 = (bf16[2,512,256]{2,1,0:T(8,128)(2,1)S(1)}, bf16[2,512,256]{2,1,0:T(8,128)(2,1)}, u32[]{:S(2)}) copy-start(bf16[2,512,256]{2,1,0:T(8,128)(2,1)} %param.15) | copy-start | bytes 1572868
  7.8 0.7 copy-start.4
  59.5 1.0 %copy-start.3 = (f32[3,8,128]{2,1,0:T(8,128)S(1)}, f32[3,8,128]{2,1,0:T(8,128)}, u32[]{:S(2)}) copy-start(f32[3,8,128]{2,1,0:T(8,128)} %get-tuple-element.8) | copy-start | bytes 36868
  80.7 1.1 %copy-start.2 = (bf16[256,16]{0,1:T(8,128)(2,1)S(1)}, bf16[256,16]{0,1:T(8,128)(2,1)}, u32[]{:S(2)}) copy-start(bf16[256,16]{0,1:T(8,128)(2,1)} %param.16) | copy-start | bytes 24580

commit v3 on v2

--- a/solution.py
+++ b/solution.py
@@ -340,15 +340,29 @@
 
 def mesh_kernel(
     planes,
-    params_ref,
-    given_ref,
+    gradient_scale,
+    amplitude_ref,
+    smoothing_ref,
+    screening_ref,
+    counts_ref,
+    features_ref,
+    cotangent_ref,
+    charge_ref,
+    message_weight_ref,
+    bases_ref,
+    offsets_ref,
     hartley_ref,
     depth_ref,
     back_ref,
-    returned_ref,
-    terms_ref,
+    message_ref,
+    gradient_ref,
+    totals_ref,
+    given_ref,
     atoms_ref,
     values_ref,
+    returned_ref,
+    parts_ref,
+    landed_ref,
     atom_planes,
     atom_columns,
     mesh,
@@ -357,11 +371,55 @@
     receive_sems,
     back_sems,
     return_sems,
+    part_sems,
+    land_sems,
+    spread_sems,
+    total_sems,
 ):
     groups, cells, unused, atoms = given_ref.shape
+    blocks = counts_ref.shape[1]
+    block_atoms = atoms // blocks
+    width = 128
     lanes = 2 * M
     own = lax.axis_index("seq")
-    greet_peers(groups, own)
+    barrier = greet_peers(groups, own)
+    slot = lax.broadcasted_iota(jnp.int32, (1, atoms), 1)
+    live = []
+    for cell in range(cells):
+        mask = jnp.zeros((1, atoms), jnp.float32)
+        for block in range(blocks):
+            first = block * block_atoms
+            held = (slot >= first) & (slot < first + counts_ref[cell, block])
+            mask = jnp.where(held, 1.0, mask)
+        live.append(mask)
+        projected = lax.dot_general(
+            charge_ref[...],
+            features_ref[cell],
+            (((0,), (1,)), ((), ())),
+            preferred_element_type=jnp.float32,
+        )
+        pulled = lax.dot_general(
+            message_weight_ref[...],
+            cotangent_ref[cell],
+            (((1,), (1,)), ((), ())),
+            preferred_element_type=jnp.float32,
+        )
+        places = jnp.concatenate(
+            [
+                bases_ref[cell].astype(jnp.float32),
+                offsets_ref[cell],
+                jnp.zeros((2, atoms), jnp.float32),
+            ],
+            axis=0,
+        )
+        given_ref[:, cell] = placed_rows(
+            [
+                (6, (projected * mask).astype(jnp.bfloat16).astype(jnp.float32)),
+                (7, (pulled * mask).astype(jnp.bfloat16).astype(jnp.float32)),
+            ],
+            jnp.broadcast_to(places[None], (groups, 8, atoms)),
+        )
+    pl.semaphore_wait(barrier, groups - 1)
 
     def send_atoms(step, carry):
         peer = lax.rem(own + step, groups)
@@ -421,9 +479,9 @@
 
     lax.fori_loop(0, groups, spread_group, 0)
 
-    amplitude = params_ref[0]
-    widths = params_ref[1]
-    screens = params_ref[2]
+    amplitude = amplitude_ref[own]
+    widths = smoothing_ref[own] * smoothing_ref[own]
+    screens = screening_ref[own] * screening_ref[own]
     plane_squares = wave_squares(
         lax.broadcasted_iota(jnp.int32, (M, lanes), 0)
     ) + wave_squares(lax.broadcasted_iota(jnp.int32, (M, lanes), 1) & (M - 1))
@@ -459,8 +517,10 @@
 
     zero = jnp.zeros((8, lanes), jnp.float32)
     sums = lax.fori_loop(0, M, filter_row, (zero, zero, zero), unroll=4)
-    for order_index in range(3):
-        terms_ref[order_index] = sums[order_index]
+    own_terms = [
+        jnp.sum(jnp.sum(total, axis=0, keepdims=True), axis=1, keepdims=True) * factor
+        for total, factor in zip(sums, (0.5, -0.5 * widths, -screens))
+    ]
 
     def read_group(step, carry):
         group = lax.rem(own + step, groups)
@@ -479,7 +539,7 @@
                 preferred_element_type=jnp.float32,
             )
             weighted = inner.reshape(2, M, atoms) * atom_columns[group, cell][None]
-            values_ref[group, cell] = jnp.sum(weighted, axis=1)
+            values_ref[group, 2 * cell : 2 * cell + 2] = jnp.sum(weighted, axis=1)
 
         @pl.when(step < groups)
         def give_back():
@@ -506,37 +566,102 @@
 
     lax.fori_loop(1, groups, finish, 0)
 
-
-def mesh_of_channel(params, atom_blocks):
-    groups, cells, unused, atoms = atom_blocks.shape
-    planes = M // groups
-    tables = stacked_tables(planes)
-    sems = pltpu.SemaphoreType.DMA((groups,))
-    whole = pl.BlockSpec(memory_space=pltpu.VMEM)
-    return pl.pallas_call(
-        functools.partial(mesh_kernel, planes),
-        out_shape=(
-            jax.ShapeDtypeStruct((groups, cells, 2, atoms), jnp.float32),
-            jax.ShapeDtypeStruct((3, 8, 2 * M), jnp.float32),
-        ),
-        in_specs=[pl.BlockSpec(memory_space=pltpu.SMEM)] + [whole] * 4,
-        out_specs=(whole, whole),
-        scratch_shapes=[
-            pltpu.VMEM(atom_blocks.shape, jnp.float32),
-            pltpu.VMEM((groups, cells, 2, atoms), jnp.float32),
-            pltpu.VMEM((groups, cells, M * 8, atoms), jnp.bfloat16),
-            pltpu.VMEM((groups, cells, M, atoms), jnp.float32),
-            pltpu.VMEM((M, groups * 8, cells * 2 * M), jnp.float32),
-            pltpu.VMEM((M, 2 * M), jnp.float32),
-            sems,
-            sems,
-            sems,
-            sems,
+    returned = jnp.concatenate([returned_ref[index] for index in range(groups)], axis=0).astype(
+        jnp.bfloat16
+    )
+    kinds = 2 * cells
+    picked_row = lax.broadcasted_iota(jnp.int32, (groups, groups * kinds), 1)
+    channel_row = lax.broadcasted_iota(jnp.int32, (groups, groups * kinds), 0) * kinds
+
+    def kind_of(cell, kind):
+        picker = jnp.where(picked_row == channel_row + (2 * cell + kind), 1.0, 0.0)
+        picked = jnp.dot(
+            picker.astype(jnp.bfloat16), returned, preferred_element_type=jnp.float32
+        )
+        return (picked * live[cell]).astype(jnp.bfloat16)
+
+    potentials = [kind_of(cell, 0) for cell in range(cells)]
+    responses = [kind_of(cell, 1) for cell in range(cells)]
+    gradient_in = jnp.zeros((groups, features_ref.shape[2]), jnp.float32)
+    gradient_out = gradient_in
+    for cell in range(cells):
+        gradient_in = gradient_in + jnp.dot(
+            responses[cell], features_ref[cell], preferred_element_type=jnp.float32
+        )
+        gradient_out = gradient_out + jnp.dot(
+            potentials[cell], cotangent_ref[cell], preferred_element_type=jnp.float32
+        )
+    parts_ref[...] = placed_rows(
+        [
+            (0, gradient_in[:, :width]),
+            (1, gradient_in[:, width:]),
+            (2, gradient_out[:, :width]),
+            (3, gradient_out[:, width:]),
         ],
-        compiler_params=pltpu.CompilerParams(
-            collective_id=0, has_side_effects=True, vmem_limit_bytes=56 * 1024 * 1024
-        ),
-    )(params, atom_blocks, *tables)
+        jnp.zeros(parts_ref.shape, jnp.float32),
+    )
+
+    def send_parts(step, carry):
+        peer = lax.rem(own + step, groups)
+        to_peer(
+            parts_ref.at[peer], landed_ref.at[own], part_sems, land_sems, peer, own
+        ).start()
+        return carry
+
+    lax.fori_loop(1, groups, send_parts, 0)
+    for cell in range(cells):
+        message_ref[cell] = lax.dot_general(
+            potentials[cell],
+            message_weight_ref[...],
+            (((0,), (0,)), ((), ())),
+            preferred_element_type=jnp.float32,
+        ).astype(jnp.bfloat16)
+        gradient_ref[cell] = lax.dot_general(
+            responses[cell],
+            charge_ref[...],
+            (((0,), (1,)), ((), ())),
+            preferred_element_type=jnp.float32,
+        ).astype(jnp.bfloat16)
+    row_index = lax.broadcasted_iota(jnp.int32, (8, width), 0)
+    lane_index = lax.broadcasted_iota(jnp.int32, (8, width), 1)
+    fixed = jnp.zeros((8, width), jnp.float32)
+    for order_index in range(3):
+        fixed = jnp.where(
+            (row_index == 4) & (lane_index == order_index), own_terms[order_index], fixed
+        )
+
+    def gather_parts(step, total):
+        peer = lax.rem(own + groups - step, groups)
+        copy = to_peer(
+            parts_ref.at[peer], landed_ref.at[peer], part_sems, land_sems, peer, peer
+        )
+        copy.wait_send()
+        copy.wait_recv()
+        return total + landed_ref[peer]
+
+    totals_ref[own] = (
+        lax.fori_loop(1, groups, gather_parts, parts_ref[own] + fixed) * gradient_scale
+    )
+
+    def spread_totals(step, carry):
+        peer = lax.rem(own + step, groups)
+        to_peer(
+            totals_ref.at[own], totals_ref.at[own], spread_sems, total_sems, peer, own
+        ).start()
+        return carry
+
+    lax.fori_loop(1, groups, spread_totals, 0)
+
+    def finish_totals(step, carry):
+        peer = lax.rem(own + groups - step, groups)
+        copy = to_peer(
+            totals_ref.at[own], totals_ref.at[peer], spread_sems, total_sems, peer, peer
+        )
+        copy.wait_send()
+        copy.wait_recv()
+        return carry
+
+    lax.fori_loop(1, groups, finish_totals, 0)
 
 
 def to_peer(source, target, send_sems, receive_sems, peer, sender):
@@ -563,62 +688,14 @@
         return carry
 
     lax.fori_loop(1, count, greet, 0)
-    pl.semaphore_wait(barrier, count - 1)
-
-
-def total_kernel(
-    count, given_ref, fixed_ref, totals_ref, landed, send_sems, receive_sems, spread_sems, total_sems
-):
-    own = lax.axis_index("seq")
-    greet_peers(count, own)
-
-    def send(step, carry):
-        peer = lax.rem(own + step, count)
-        to_peer(given_ref.at[peer], landed.at[own], send_sems, receive_sems, peer, own).start()
-        return carry
-
-    lax.fori_loop(1, count, send, 0)
-
-    def gather(step, total):
-        peer = lax.rem(own + step, count)
-        copy = to_peer(given_ref.at[peer], landed.at[peer], send_sems, receive_sems, peer, peer)
-        copy.wait_send()
-        copy.wait_recv()
-        return total + landed[peer]
-
-    totals_ref[own] = lax.fori_loop(1, count, gather, given_ref[own] + fixed_ref[...])
-
-    def spread(step, carry):
-        peer = lax.rem(own + step, count)
-        to_peer(totals_ref.at[own], totals_ref.at[own], spread_sems, total_sems, peer, own).start()
-        return carry
-
-    lax.fori_loop(1, count, spread, 0)
-
-    def finish(step, carry):
-        peer = lax.rem(own + step, count)
-        copy = to_peer(
-            totals_ref.at[own], totals_ref.at[peer], spread_sems, total_sems, peer, peer
-        )
-        copy.wait_send()
-        copy.wait_recv()
-        return carry
-
-    lax.fori_loop(1, count, finish, 0)
-
-
-def totals_of_channels(blocks, fixed, collective_id):
-    count = blocks.shape[0]
-    whole = pl.BlockSpec(memory_space=pltpu.VMEM)
-    sems = pltpu.SemaphoreType.DMA((count,))
-    return pl.pallas_call(
-        functools.partial(total_kernel, count),
-        out_shape=jax.ShapeDtypeStruct(blocks.shape, blocks.dtype),
-        in_specs=[whole, whole],
-        out_specs=whole,
-        scratch_shapes=[pltpu.VMEM(blocks.shape, blocks.dtype), sems, sems, sems, sems],
-        compiler_params=pltpu.CompilerParams(collective_id=collective_id, has_side_effects=True),
-    )(blocks, fixed)
+    return barrier
+
+
+def placed_rows(entries, base):
+    row_index = lax.broadcasted_iota(jnp.int32, base.shape, 1)
+    for row, table in entries:
+        base = jnp.where(row_index == row, table[:, None, :], base)
+    return base
 
 
 def by_channel(
@@ -634,80 +711,58 @@
     row_starts,
     block_counts,
 ):
-    cell_count, atom_rows, features = atom_features.shape
-    channels = charge_weight.shape[1]
-    devices = lax.axis_size("seq")
-    blocks = block_counts.shape[1]
-    channel = lax.axis_index("seq")
-    slot_index = jnp.arange(atom_rows // blocks, dtype=jnp.int32)
-    live = (slot_index[None, None, :] < block_counts[:, :, None]).reshape(cell_count, atom_rows)
-    live_mask = live.astype(jnp.float32)
-    projected = lax.dot_general(
+    cells, atoms, features = atom_features.shape
+    groups = charge_weight.shape[1]
+    planes = M // groups
+    tables = stacked_tables(planes)
+    sems = pltpu.SemaphoreType.DMA((groups,))
+    whole = pl.BlockSpec(memory_space=pltpu.VMEM)
+    scalar = pl.BlockSpec(memory_space=pltpu.SMEM)
+    gradient_scale = 1.0 / math.sqrt(cells * atoms * groups)
+    atom_blocks = (groups, cells, 8, atoms)
+    value_blocks = (groups, 2 * cells, atoms)
+    part_blocks = (groups, 8, 128)
+    message, atom_gradient, totals = pl.pallas_call(
+        functools.partial(mesh_kernel, planes, gradient_scale),
+        out_shape=(
+            jax.ShapeDtypeStruct(atom_features.shape, jnp.bfloat16),
+            jax.ShapeDtypeStruct(atom_features.shape, jnp.bfloat16),
+            jax.ShapeDtypeStruct(part_blocks, jnp.float32),
+        ),
+        in_specs=[scalar] * 4 + [whole] * 9,
+        out_specs=(whole, whole, whole),
+        scratch_shapes=[
+            pltpu.VMEM(atom_blocks, jnp.float32),
+            pltpu.VMEM(atom_blocks, jnp.float32),
+            pltpu.VMEM(value_blocks, jnp.float32),
+            pltpu.VMEM(value_blocks, jnp.float32),
+            pltpu.VMEM(part_blocks, jnp.float32),
+            pltpu.VMEM(part_blocks, jnp.float32),
+            pltpu.VMEM((groups, cells, M * 8, atoms), jnp.bfloat16),
+            pltpu.VMEM((groups, cells, M, atoms), jnp.float32),
+            pltpu.VMEM((M, groups * 8, cells * 2 * M), jnp.float32),
+            pltpu.VMEM((M, 2 * M), jnp.float32),
+        ]
+        + [sems] * 8,
+        compiler_params=pltpu.CompilerParams(
+            collective_id=0, has_side_effects=True, vmem_limit_bytes=56 * 1024 * 1024
+        ),
+    )(
+        amplitude,
+        smoothing,
+        screening,
+        block_counts,
+        atom_features,
+        cotangent,
         charge_weight,
-        atom_features,
-        (((0,), (2,)), ((), ())),
-        preferred_element_type=jnp.float32,
-    )
-    pulled = lax.dot_general(
-        message_weight, cotangent, (((1,), (2,)), ((), ())), preferred_element_type=jnp.float32
-    )
-    charges = (jnp.stack([projected, pulled], axis=2) * live_mask[None, :, None, :]).astype(
-        jnp.bfloat16
-    )
-    places = jnp.concatenate([base_cells.astype(jnp.float32), cell_offsets], axis=1)
-    blocks_out = jnp.concatenate(
-        [
-            jnp.broadcast_to(places[None], (devices,) + places.shape),
-            charges.astype(jnp.float32),
-        ],
-        axis=2,
-    )
-    params = lax.dynamic_slice_in_dim(
-        jnp.stack([amplitude, smoothing * smoothing, screening * screening]), channel, 1, 1
-    ).reshape(3)
-    returned, sums = mesh_of_channel(params, blocks_out)
-    returned = returned.astype(jnp.bfloat16)
-    potential = returned[:, :, 0]
-    response = jnp.where(live[None], returned[:, :, 1], jnp.zeros((), jnp.bfloat16))
-    outgoing = lax.dot_general(
-        potential, message_weight, (((0,), (0,)), ((), ())), preferred_element_type=jnp.float32
-    )
-    message = (live_mask[:, :, None] * outgoing).astype(jnp.bfloat16)
-    atom_gradient = lax.dot_general(
-        response, charge_weight, (((0,), (1,)), ((), ())), preferred_element_type=jnp.float32
-    ).astype(jnp.bfloat16)
-    gradient_scale = 1.0 / math.sqrt(cell_count * atom_rows * devices)
-    live_potential = jnp.where(live[None], potential, jnp.zeros((), jnp.bfloat16))
-    gradient_in = lax.dot_general(
-        response,
-        atom_features,
-        (((1, 2), (0, 1)), ((), ())),
-        preferred_element_type=jnp.float32,
-    )
-    gradient_out = lax.dot_general(
-        live_potential,
-        cotangent,
-        (((1, 2), (0, 1)), ((), ())),
-        preferred_element_type=jnp.float32,
-    )
-    factors = jnp.stack([jnp.ones((), jnp.float32), -params[1], -2.0 * params[2]])
-    own_terms = jnp.sum(sums, axis=(1, 2)) * factors * 0.5
-    width = 128
-    rows = features // width
-    padding = 8 - 2 * rows
-    blocks_out = jnp.concatenate(
-        [
-            gradient_in.reshape(channels, rows, width),
-            gradient_out.reshape(channels, rows, width),
-            jnp.zeros((channels, padding, width), jnp.float32),
-        ],
-        axis=1,
-    )
-    fixed = jnp.pad(own_terms[None, :], ((2 * rows, padding - 1), (0, width - 3)))
-    totals = totals_of_channels(blocks_out, fixed, 1) * gradient_scale
-    gradient_in = totals[:, :rows].reshape(channels, features).T
-    gradient_out = totals[:, rows : 2 * rows].reshape(channels, features)
-    filter_terms = totals[:, 2 * rows, :3].T
+        message_weight,
+        base_cells,
+        cell_offsets,
+        *tables,
+    )
+    gradient_in = totals[:, 0:2].reshape(groups, features).T
+    gradient_out = totals[:, 2:4].reshape(groups, features)
+    filter_terms = totals[:, 4, :3].T
     return (message, atom_gradient, gradient_in, gradient_out, filter_terms)
 
 

time: 83.4 us -> 70.4 us (0.84)
  other arithmetic: 6.78 us -> 0 us
  Pallas kernels: 64.8 us -> 60.8 us
  matrix products: 3.79 us -> 0 us
  local copies, waits for them, and re-layouts: 5.43 us -> 8.53 us
  between operations: 2.1 us -> 0.66 us
    pallas_call x2 -> x1, Pallas kernels: 64.8 us -> 60.8 us  [by_channel(): pl.pallas_call(functools.partial(mesh_kernel, planes, gradient_scale), ou...]
    dot_general x6 -> x0, matrix products: 3.79 us -> none  [the longest x1 1.14 us: by_channel(): lax.dot_general(response, charge_weight, (((0,), (1,)), ((), ())), prefer...]
    unnamed x13 -> x11, local copies, waits for them, and re-layouts: 2.6 us -> 5.49 us
    concatenate x3 -> x0, other arithmetic: 2.33 us -> none  [the longest x1 0.9 us: by_channel(): jnp.concatenate([jnp.broadcast_to(places[None], (devices,) + places.shape...]
    convert_element_type x4 -> x0, other arithmetic: 1.81 us -> none  [the longest x1 0.96 us: by_channel(): returned = returned.astype(jnp.bfloat16)]
    another operation x2 -> x0, other arithmetic: 1.41 us -> none  [by_channel(): jnp.stack([amplitude, smoothing * smoothing, screening * screening])]
    slice x4 -> x3, local copies, waits for them, and re-layouts: 1.19 us -> 2.43 us  [the longest x2 1.5 us: by_channel(): filter_terms = totals[:, 4, :3].T]
    mul x2 -> x0, other arithmetic: 0.93 us -> none  [the longest x1 0.85 us: by_channel(): totals = totals_of_channels(blocks_out, fixed, 1) * gradient_scale]
where the time goes in v3:
time: 70.4 us; the launch traced here: 70 us
  Pallas kernels  60.8 us (86%)
  local copies, waits for them, and re-layouts  8.53 us (12%)
    pallas_call x1, Pallas kernels, by_channel(): pl.pallas_call(functools.partial(mesh_kernel, planes, gradient_scale), ou...  60.8 us
    unnamed x11, local copies, waits for them, and re-layouts  5.49 us
    slice x2, local copies, waits for them, and re-layouts, by_channel(): filter_terms = totals[:, 4, :3].T  1.5 us

profile of v3, /device:TPU:0, one launch (start us, length us, event | category | flops | bytes accessed | tf_op | source)
XLA Modules:
  0.0 70.0 jit_solution(502259560660726309)
XLA Ops:
  0.6 0.0 copy-start.1
  0.6 1.4 %copy.18.charge_ref = bf16[256,16]{1,0:T(8,128)(2,1)} copy(bf16[256,16]{0,1:T(8,128)(2,1)} %param.16) | data formatting | bytes 16384 | tf_op args[2]
  2.1 0.0 copy-done.1
  2.1 0.0 copy-start.2
  2.1 0.6 copy.19.bases_ref
  2.7 0.1 copy-done.2
  2.8 0.6 copy.20.offsets_ref
  3.4 60.8 %shard_map.164 = (bf16[2,512,256]{2,1,0:T(8,128)(2,1)}, bf16[2,512,256]{2,1,0:T(8,128)(2,1)}, f32[16,8,128]{2,1,0:T(8,128)}) custom-call(f32[16]{0:T(128)} %amplitude_ref.1, f32[16]{0:T(128)} %smoothing_ref.1, f32[16]{0:T(128)} %screening_ref.1, s32[2,4]{1,0:T(2,128)} %counts_ref.1, bf16[2,512,256]{2,1,0:T(8,128)(2,1)} %features_ref.1, ...), custom_call_target="tpu_custom_call" | custom-call | tf_op jit(solution)/shard_map/pallas_call | solution.py:725
  64.3 0.9 %fusion = (f32[16,2,128]{2,1,0:T(2,128)S(1)}, f32[16,2,128]{2,1,0:T(2,128)S(1)}) fusion(f32[16,8,128]{2,1,0:T(8,128)} %get-tuple-element.10), kind=kLoop, calls=%fused_computation.2 | loop fusion | bytes 65536 | tf_op jit(solution)/shard_map/slice | solution.py:764
  65.2 0.6 copy_bitcast_fusion
  65.8 0.8 %slice.11 = f32[16,1,3]{2,1,0:T(1,128)S(1)} slice(f32[16,8,128]{2,1,0:T(8,128)} %get-tuple-element.10), slice={[0:16], [4:5], [0:3]} | slice | bytes 384 | tf_op jit(solution)/shard_map/slice | solution.py:765
  66.6 0.7 copy.21
  67.3 0.0 copy-start
  67.3 1.9 %copy.28 = bf16[2,512,256]{2,1,0:T(8,128)(2,1)} copy(bf16[2,512,256]{2,1,0:T(8,128)(2,1)} %get-tuple-element.20) | data formatting | bytes 1048576
  69.2 0.0 copy-done
  69.2 0.8 %copy.29 = bf16[2,512,256]{2,1,0:T(8,128)(2,1)} copy(bf16[2,512,256]{2,1,0:T(8,128)(2,1)S(1)} %copy-done) | data formatting | bytes 1048576
Async XLA Ops:
  0.6 1.4 %copy-start.1 = (s32[2,3,512]{2,0,1:T(2,128)S(1)}, s32[2,3,512]{2,0,1:T(2,128)}, u32[]{:S(2)}) copy-start(s32[2,3,512]{2,0,1:T(2,128)} %param.21) | copy-start | bytes 36868
  2.1 0.7 %copy-start.2 = (f32[2,3,512]{2,0,1:T(2,128)S(1)}, f32[2,3,512]{2,0,1:T(2,128)}, u32[]{:S(2)}) copy-start(f32[2,3,512]{2,0,1:T(2,128)} %param.22) | copy-start | bytes 36868
  67.3 1.9 %copy-start = (bf16[2,512,256]{2,1,0:T(8,128)(2,1)S(1)}, bf16[2,512,256]{2,1,0:T(8,128)(2,1)}, u32[]{:S(2)}) copy-start(bf16[2,512,256]{2,1,0:T(8,128)(2,1)} %get-tuple-element.21) | copy-start | bytes 1572868

commit v4 on v3

--- a/solution.py
+++ b/solution.py
@@ -322,9 +322,11 @@
     def parts(table):
         high = table.astype(ml_dtypes.bfloat16)
         low = (table - high.astype(np.float32)).astype(ml_dtypes.bfloat16)
-        return jnp.asarray(np.concatenate([high, high, low], axis=1))
-
-    return (parts(hartley), parts(depth), parts(depth.T))
+        return np.concatenate([high, high, low], axis=1)
+
+    high, unused, low = np.split(parts(depth), 3, axis=1)
+    stacked_depth = np.concatenate([high, low], axis=0)
+    return tuple(jnp.asarray(table) for table in (parts(hartley), stacked_depth, parts(depth.T)))
 
 
 def stacked_parts(value):
@@ -395,7 +397,7 @@
         projected = lax.dot_general(
             charge_ref[...],
             features_ref[cell],
-            (((0,), (1,)), ((), ())),
+            (((1,), (1,)), ((), ())),
             preferred_element_type=jnp.float32,
         )
         pulled = lax.dot_general(
@@ -406,8 +408,8 @@
         )
         places = jnp.concatenate(
             [
-                bases_ref[cell].astype(jnp.float32),
-                offsets_ref[cell],
+                *(bases_ref[way, cell : cell + 1].astype(jnp.float32) for way in range(3)),
+                *(offsets_ref[way, cell : cell + 1] for way in range(3)),
                 jnp.zeros((2, atoms), jnp.float32),
             ],
             axis=0,
@@ -431,15 +433,7 @@
     lax.fori_loop(1, groups, send_atoms, 0)
     atoms_ref[own] = given_ref[own]
 
-    def spread_group(step, carry):
-        group = lax.rem(own + groups - step, groups)
-
-        @pl.when(step > 0)
-        def arrive():
-            to_peer(
-                given_ref.at[group], atoms_ref.at[group], send_sems, receive_sems, group, group
-            ).wait_recv()
-
+    def spread_group(group):
         for cell in range(cells):
             places = atoms_ref[group, cell]
             fractions = spline_weights(places[3:6])
@@ -475,9 +469,24 @@
             mesh[:, pl.ds(pl.multiple_of(group * 8, 8), 8), cell * lanes : (cell + 1) * lanes] = (
                 added.reshape(M, 8, lanes)
             )
+
+    spread_group(own)
+    together = 3 if groups % 3 == 1 else 1
+
+    def spread_groups(step, carry):
+        arrived = [
+            lax.rem(own + groups - (1 + step * together + ahead), groups)
+            for ahead in range(together)
+        ]
+        for group in arrived:
+            to_peer(
+                given_ref.at[group], atoms_ref.at[group], send_sems, receive_sems, group, group
+            ).wait_recv()
+        for group in arrived:
+            spread_group(group)
         return carry
 
-    lax.fori_loop(0, groups, spread_group, 0)
+    lax.fori_loop(0, (groups - 1) // together, spread_groups, 0)
 
     amplitude = amplitude_ref[own]
     widths = smoothing_ref[own] * smoothing_ref[own]
@@ -488,9 +497,10 @@
     plane_gains[...] = (amplitude * (1.0 / M**3)) * jnp.exp((-0.5 * widths) * plane_squares)
 
     def filter_row(row, sums):
-        spectrum = jnp.dot(
-            depth_ref[...], stacked_parts(mesh[row]), preferred_element_type=jnp.float32
-        )
+        both = jnp.dot(
+            depth_ref[...], mesh[row].astype(jnp.bfloat16), preferred_element_type=jnp.float32
+        )
+        spectrum = both[:M] + both[M:]
         signed = jnp.where(row < M // 2, row, row - M).astype(jnp.float32)
         row_square = signed * signed * ((2.0 * math.pi / M) ** 2)
         squares = plane_squares + row_square
@@ -516,14 +526,13 @@
         )
 
     zero = jnp.zeros((8, lanes), jnp.float32)
-    sums = lax.fori_loop(0, M, filter_row, (zero, zero, zero), unroll=4)
+    sums = lax.fori_loop(0, M, filter_row, (zero, zero, zero), unroll=8)
     own_terms = [
         jnp.sum(jnp.sum(total, axis=0, keepdims=True), axis=1, keepdims=True) * factor
         for total, factor in zip(sums, (0.5, -0.5 * widths, -screens))
     ]
 
-    def read_group(step, carry):
-        group = lax.rem(own + step, groups)
+    def read_group(group):
         for cell in range(cells):
             window = (
                 mesh[
@@ -541,15 +550,20 @@
             weighted = inner.reshape(2, M, atoms) * atom_columns[group, cell][None]
             values_ref[group, 2 * cell : 2 * cell + 2] = jnp.sum(weighted, axis=1)
 
-        @pl.when(step < groups)
-        def give_back():
+    def read_groups(step, carry):
+        asked = [
+            lax.rem(own + (1 + step * together + ahead), groups) for ahead in range(together)
+        ]
+        for group in asked:
+            read_group(group)
+        for group in asked:
             to_peer(
                 values_ref.at[group], returned_ref.at[own], back_sems, return_sems, group, own
             ).start()
-
         return carry
 
-    lax.fori_loop(1, groups + 1, read_group, 0)
+    lax.fori_loop(0, (groups - 1) // together, read_groups, 0)
+    read_group(own)
     returned_ref[own] = values_ref[own]
 
     def finish(step, carry):
@@ -619,7 +633,7 @@
         gradient_ref[cell] = lax.dot_general(
             responses[cell],
             charge_ref[...],
-            (((0,), (1,)), ((), ())),
+            (((0,), (0,)), ((), ())),
             preferred_element_type=jnp.float32,
         ).astype(jnp.bfloat16)
     row_index = lax.broadcasted_iota(jnp.int32, (8, width), 0)
@@ -754,10 +768,10 @@
         block_counts,
         atom_features,
         cotangent,
-        charge_weight,
+        charge_weight.T,
         message_weight,
-        base_cells,
-        cell_offsets,
+        jnp.swapaxes(base_cells, 0, 1),
+        jnp.swapaxes(cell_offsets, 0, 1),
         *tables,
     )
     gradient_in = totals[:, 0:2].reshape(groups, features).T

time: 70.4 us -> 56.1 us (0.80)
  Pallas kernels: 60.8 us -> 49.4 us
  local copies, waits for them, and re-layouts: 8.53 us -> 5.77 us
    pallas_call x1, Pallas kernels: 60.8 us -> 49.4 us  [by_channel(): pl.pallas_call(functools.partial(mesh_kernel, planes, gradient_scale), ou...]
    unnamed x11 -> x4, local copies, waits for them, and re-layouts: 5.49 us -> 2.72 us
where the time goes in v4:
time: 56.1 us; the launch traced here: 55.8 us
  Pallas kernels  49.4 us (88%)
  local copies, waits for them, and re-layouts  5.77 us (10%)
  between operations  0.65 us (1%)
    pallas_call x1, Pallas kernels, by_channel(): pl.pallas_call(functools.partial(mesh_kernel, planes, gradient_scale), ou...  49.4 us
    unnamed x4, local copies, waits for them, and re-layouts  2.72 us
    slice x2, local copies, waits for them, and re-layouts, by_channel(): filter_terms = totals[:, 4, :3].T  1.5 us

profile of v4, /device:TPU:0, one launch (start us, length us, event | category | flops | bytes accessed | tf_op | source)
XLA Modules:
  0.0 55.8 jit_solution(12610582362925015696)
XLA Ops:
  0.6 49.4 %shard_map.164 = (bf16[2,512,256]{2,1,0:T(8,128)(2,1)}, bf16[2,512,256]{2,1,0:T(8,128)(2,1)}, f32[16,8,128]{2,1,0:T(8,128)}) custom-call(f32[16]{0:T(128)} %amplitude_ref.1, f32[16]{0:T(128)} %smoothing_ref.1, f32[16]{0:T(128)} %screening_ref.1, s32[2,4]{1,0:T(2,128)} %counts_ref.1, bf16[2,512,256]{2,1,0:T(8,128)(2,1)} %features_ref.1, ...), custom_call_target="tpu_custom_call" | custom-call | tf_op jit(solution)/shard_map/pallas_call | solution.py:739
  50.0 0.9 %fusion = (f32[16,2,128]{2,1,0:T(2,128)S(1)}, f32[16,2,128]{2,1,0:T(2,128)S(1)}) fusion(f32[16,8,128]{2,1,0:T(8,128)} %get-tuple-element.10), kind=kLoop, calls=%fused_computation.2 | loop fusion | bytes 65536 | tf_op jit(solution)/shard_map/slice | solution.py:778
  51.0 0.6 %copy_bitcast_fusion = (f32[16,256]{1,0:T(8,128)}, f32[256,16]{0,1:T(8,128)}) fusion(f32[2,8,2,128]{3,2,1,0:T(2,128)S(1)} %bitcast.14, f32[2,8,2,128]{3,2,1,0:T(2,128)S(1)} %bitcast.15), kind=kLoop, calls=%fused_computation | loop fusion | bytes 65536 | tf_op jit(solution)/shard_map/reshape | solution.py:778
  51.6 0.8 %slice.11 = f32[16,1,3]{2,1,0:T(1,128)S(1)} slice(f32[16,8,128]{2,1,0:T(8,128)} %get-tuple-element.10), slice={[0:16], [4:5], [0:3]} | slice | bytes 384 | tf_op jit(solution)/shard_map/slice | solution.py:779
  52.4 0.7 %copy.18 = f32[16,1,3]{0,2,1:T(4,128)} copy(f32[16,1,3]{2,1,0:T(1,128)S(1)} %slice.11) | data formatting | bytes 384 | tf_op jit(solution)/shard_map/slice | solution.py:779
  53.1 0.0 copy-start
  53.1 1.9 %copy.25 = bf16[2,512,256]{2,1,0:T(8,128)(2,1)} copy(bf16[2,512,256]{2,1,0:T(8,128)(2,1)} %get-tuple-element.20) | data formatting | bytes 1048576
  55.0 0.0 copy-done
  55.0 0.8 %copy.26 = bf16[2,512,256]{2,1,0:T(8,128)(2,1)} copy(bf16[2,512,256]{2,1,0:T(8,128)(2,1)S(1)} %copy-done) | data formatting | bytes 1048576
Async XLA Ops:
  53.1 1.9 %copy-start = (bf16[2,512,256]{2,1,0:T(8,128)(2,1)S(1)}, bf16[2,512,256]{2,1,0:T(8,128)(2,1)}, u32[]{:S(2)}) copy-start(bf16[2,512,256]{2,1,0:T(8,128)(2,1)} %get-tuple-element.21) | copy-start | bytes 1572868

commit v5 on v4

--- a/solution.py
+++ b/solution.py
@@ -358,6 +358,9 @@
     back_ref,
     message_ref,
     gradient_ref,
+    gradient_in_ref,
+    gradient_out_ref,
+    filter_ref,
     totals_ref,
     given_ref,
     atoms_ref,
@@ -526,7 +529,7 @@
         )
 
     zero = jnp.zeros((8, lanes), jnp.float32)
-    sums = lax.fori_loop(0, M, filter_row, (zero, zero, zero), unroll=8)
+    sums = lax.fori_loop(0, M, filter_row, (zero, zero, zero), unroll=16)
     own_terms = [
         jnp.sum(jnp.sum(total, axis=0, keepdims=True), axis=1, keepdims=True) * factor
         for total, factor in zip(sums, (0.5, -0.5 * widths, -screens))
@@ -676,6 +679,11 @@
         return carry
 
     lax.fori_loop(1, groups, finish_totals, 0)
+    gradient_in_ref[:, :width] = totals_ref[:, 0, :]
+    gradient_in_ref[:, width:] = totals_ref[:, 1, :]
+    gradient_out_ref[:, :width] = totals_ref[:, 2, :]
+    gradient_out_ref[:, width:] = totals_ref[:, 3, :]
+    filter_ref[...] = totals_ref[:, 4, :]
 
 
 def to_peer(source, target, send_sems, receive_sems, peer, sender):
@@ -736,16 +744,19 @@
     atom_blocks = (groups, cells, 8, atoms)
     value_blocks = (groups, 2 * cells, atoms)
     part_blocks = (groups, 8, 128)
-    message, atom_gradient, totals = pl.pallas_call(
+    message, atom_gradient, gradient_in, gradient_out, filter_rows = pl.pallas_call(
         functools.partial(mesh_kernel, planes, gradient_scale),
         out_shape=(
             jax.ShapeDtypeStruct(atom_features.shape, jnp.bfloat16),
             jax.ShapeDtypeStruct(atom_features.shape, jnp.bfloat16),
-            jax.ShapeDtypeStruct(part_blocks, jnp.float32),
+            jax.ShapeDtypeStruct((groups, features), jnp.float32),
+            jax.ShapeDtypeStruct((groups, features), jnp.float32),
+            jax.ShapeDtypeStruct((groups, 128), jnp.float32),
         ),
         in_specs=[scalar] * 4 + [whole] * 9,
-        out_specs=(whole, whole, whole),
+        out_specs=(whole,) * 5,
         scratch_shapes=[
+            pltpu.VMEM(part_blocks, jnp.float32),
             pltpu.VMEM(atom_blocks, jnp.float32),
             pltpu.VMEM(atom_blocks, jnp.float32),
             pltpu.VMEM(value_blocks, jnp.float32),
@@ -774,10 +785,7 @@
         jnp.swapaxes(cell_offsets, 0, 1),
         *tables,
     )
-    gradient_in = totals[:, 0:2].reshape(groups, features).T
-    gradient_out = totals[:, 2:4].reshape(groups, features)
-    filter_terms = totals[:, 4, :3].T
-    return (message, atom_gradient, gradient_in, gradient_out, filter_terms)
+    return (message, atom_gradient, gradient_in.T, gradient_out, filter_rows[:, :3].T)
 
 
 def solution(mesh):

time: 56.1 us -> 54.7 us (0.975)
  Pallas kernels: 49.4 us -> 48.3 us
    unnamed x4 -> x13, local copies, waits for them, and re-layouts: 2.72 us -> 5.4 us
    slice x3 -> x0, local copies, waits for them, and re-layouts: 2.43 us -> none  [the longest x2 1.5 us: by_channel(): filter_terms = totals[:, 4, :3].T]
    pallas_call x1, Pallas kernels: 49.4 us -> 48.3 us  [by_channel(): pl.pallas_call(functools.partial(mesh_kernel, planes, gradient_scale), ou...]
    reshape x1 -> x0, local copies, waits for them, and re-layouts: 0.62 us -> none  [by_channel(): gradient_out = totals[:, 2:4].reshape(groups, features)]
where the time goes in v5:
time: 54.7 us; the launch traced here: 54.4 us
  Pallas kernels  48.3 us (88%)
  local copies, waits for them, and re-layouts  5.4 us (10%)
  between operations  0.66 us (1%)
    pallas_call x1, Pallas kernels, by_channel(): pl.pallas_call(functools.partial(mesh_kernel, planes, gradient_scale), ou...  48.3 us
    unnamed x13, local copies, waits for them, and re-layouts  5.4 us

profile of v5, /device:TPU:0, one launch (start us, length us, event | category | flops | bytes accessed | tf_op | source)
XLA Modules:
  0.0 54.4 jit_solution(17726662268046796326)
XLA Ops:
  0.6 48.3 %shard_map.164 = (bf16[2,512,256]{2,1,0:T(8,128)(2,1)}, bf16[2,512,256]{2,1,0:T(8,128)(2,1)}, f32[16,256]{1,0:T(8,128)}, f32[16,256]{1,0:T(8,128)}, f32[16,128]{1,0:T(8,128)}) custom-call(f32[16]{0:T(128)} %amplitude_ref.1, f32[16]{0:T(128)} %smoothing_ref.1, f32[16]{0:T(128)} %screening_ref.1, s32[2,4]{1,0:T(2,128)} %counts_ref.1, ...), custom_call_target="tpu_custom_call" | custom-call | tf_op jit(solution)/shard_map/pallas_call | solution.py:747
  48.9 0.0 copy-start.3
  48.9 0.7 %copy-done.3 = f32[16,128]{1,0:T(8,128)S(1)} copy-done((f32[16,128]{1,0:T(8,128)S(1)}, f32[16,128]{1,0:T(8,128)}, u32[]{:S(2)}) %copy-start.3) | copy-done | bytes 8216
  49.6 0.7 %copy.18 = f32[3,16]{1,0:T(4,128)} copy(f32[3,16]{0,1:T(8,128)S(1)} %slice_bitcast_fusion) | data formatting | bytes 384
  50.3 0.0 copy-start
  50.3 1.9 %copy.23 = bf16[2,512,256]{2,1,0:T(8,128)(2,1)} copy(bf16[2,512,256]{2,1,0:T(8,128)(2,1)} %get-tuple-element.25) | data formatting | bytes 1048576
  52.2 0.0 copy-done
  52.2 0.0 copy-start.2
  52.2 0.8 %copy.24 = bf16[2,512,256]{2,1,0:T(8,128)(2,1)} copy(bf16[2,512,256]{2,1,0:T(8,128)(2,1)S(1)} %copy-done) | data formatting | bytes 1048576
  53.0 0.0 copy-done.2
  53.0 0.0 copy-start.1
  53.0 0.6 %copy.25 = f32[256,16]{0,1:T(8,128)} copy(f32[256,16]{0,1:T(8,128)S(1)} %bitcast.6) | data formatting | bytes 32768
  53.6 0.1 copy-done.1
  53.8 0.6 %copy.26 = f32[16,256]{1,0:T(8,128)} copy(f32[16,256]{1,0:T(8,128)S(1)} %copy-done.1) | data formatting | bytes 32768
  (1 shorter events, 0.0 us)
Async XLA Ops:
  48.9 0.7 %copy-start.3 = (f32[16,128]{1,0:T(8,128)S(1)}, f32[16,128]{1,0:T(8,128)}, u32[]{:S(2)}) copy-start(f32[16,128]{1,0:T(8,128)} %get-tuple-element.14) | copy-start | bytes 24580
  50.3 1.9 %copy-start = (bf16[2,512,256]{2,1,0:T(8,128)(2,1)S(1)}, bf16[2,512,256]{2,1,0:T(8,128)(2,1)}, u32[]{:S(2)}) copy-start(bf16[2,512,256]{2,1,0:T(8,128)(2,1)} %get-tuple-element.26) | copy-start | bytes 1572868
  52.2 0.8 %copy-start.2 = (f32[16,256]{1,0:T(8,128)S(1)}, f32[16,256]{1,0:T(8,128)}, u32[]{:S(2)}) copy-start(f32[16,256]{1,0:T(8,128)} %get-tuple-element.12) | copy-start | bytes 49156
  53.0 0.7 %copy-start.1 = (f32[16,256]{1,0:T(8,128)S(1)}, f32[16,256]{1,0:T(8,128)}, u32[]{:S(2)}) copy-start(f32[16,256]{1,0:T(8,128)} %get-tuple-element.28) | copy-start | bytes 49156
